TPU v7x, 32 devices: a whole 2x2x4 slice. The times are simulated.
32 devices in a mesh: cells: 16 (over z, y, x), rep: 2 (over core).
Axes of the slice: x: 2, y: 2, z: 4, core: 2. Of those that a mesh axis runs over, the one named last changes fastest.
Arguments:
- cells_x: bfloat16 [18432, 7000], P(('cells', 'rep')), may hold values from -12 to 12
- latent_noise: float32 [18432, 100], P(('cells', 'rep')), may hold values from -6 to 6
- group_ids: int32 [18432], P(('cells', 'rep')), may hold values from 0 to 63, as said below
- owner_table: int32 [16, 4], replicated, may hold values from 0 to 31, as said below
- owner_mask: int32 [16, 4], replicated, may hold values from 0 to 1
- enc_w1: bfloat16 [7000, 800], replicated, may hold values from -0.0625 to 0.0625
- enc_w2: bfloat16 [800, 800], replicated, may hold values from -0.21875 to 0.21875
- head_w: bfloat16 [800, 200], replicated, may hold values from -0.21875 to 0.21875
- head_b: float32 [200], replicated, may hold values from -3 to 3
- dec_w1: bfloat16 [100, 800], replicated, may hold values from -0.625 to 0.625
- dec_w2: bfloat16 [800, 800], replicated, may hold values from -0.21875 to 0.21875
- out_w: bfloat16 [800, 7000], replicated, may hold values from -0.109375 to 0.109375
- out_b: float32 [7000], replicated, may hold values from -0.05 to 0.05
- bn_gain: float32 [4, 800], replicated, may hold values from 0.25 to 1.75
- bn_shift: float32 [4, 800], replicated, may hold values from -0.7 to -0.3
Outputs:
- grad_x: float32 [18432, 7000], P(('cells', 'rep'))
- grad_enc_w1: float32 [6400, 875], P(('cells', 'rep'))
- grad_narrow: float32 [2048, 625], P(('cells', 'rep'))
- grad_head_w: float32 [800, 200], replicated
- grad_dec_w1: float32 [100, 800], replicated
- grad_head_b: float32 [200], replicated
- grad_out_w: float32 [6400, 875], P(('cells', 'rep'))
- grad_out_b: float32 [7000], replicated
- grad_gain: float32 [4, 800], replicated
- grad_shift: float32 [4, 800], replicated
- offsets: float32 [16, 4, 100], P('cells')
Inputs may be any that keep to these rules, and one draw needn't show every extreme that they name: `group_ids`: A cell's group is 2 * its population + its condition (1 stimulated, 0 control); populations differ in size, and some groups hold no cells. `owner_table`: each population 0 to 31 stands in exactly one live slot; a row's live slots come first and masked slots hold 0; some rows have all 4 slots live and some none.
All inputs are finite; a program needn't handle non-finite values.
Results may differ from a plain program's by a relative error of at most 0.018.
Values sent between devices are 32-bit elements; how exact they have to be, the bound alone decides.
A program may use at most 256 MiB of HBM per device.

v0:
```python
import functools

import jax
import jax.numpy as jnp
from jax import lax
from jax.experimental import pallas as pl
from jax.experimental.pallas import tpu as pltpu
from jax.sharding import PartitionSpec as P

POP_DEV = 2
FLAT_COLS = 875
NARROW_COLS = 625
FLAT_ROWS = 6400
NARROW_ROWS = 2048

NORM_EPSILON = 1e-05
KL_WEIGHT = 5e-05
OFFSET_WEIGHT = 200.0

MESH_ID = pl.DeviceIdType.MESH
WIN = 1024
ROWS = 48
F32 = jnp.float32
BF16 = jnp.bfloat16


class Slice:
    def __init__(self, cells, rep):
        self.cells, self.rep = cells, rep
        self.n = cells * rep
        self.bits = self.n.bit_length() - 1
        self.digits = []
        low = 0
        while low < self.bits:
            width = min(3, self.bits - low)
            self.digits.append((low, 1 << width))
            low += width

    def me(self):
        return lax.axis_index("cells") * self.rep + lax.axis_index("rep")

    def place(self, index):
        return (index // self.rep, index % self.rep)


def greet(grid, peers):
    barrier = pltpu.get_barrier_semaphore()
    for peer in peers:
        pl.semaphore_signal(barrier, inc=1, device_id=grid.place(peer), device_id_type=MESH_ID)


def meet(peers):
    pl.semaphore_wait(pltpu.get_barrier_semaphore(), len(peers))


def digit_peers(grid):
    me = grid.me()
    peers = []
    for low, size in grid.digits:
        rank = (me // (1 << low)) % size
        for k in range(1, size):
            other = (rank + k) % size
            peers.append(me + (other - rank) * (1 << low))
    return peers


class Gather:
    def __init__(self, grid, buffers, send_sems, recv_sems):
        self.grid, self.buffers, self.send_sems, self.recv_sems = grid, buffers, send_sems, recv_sems

    def rank(self, level):
        low, size = self.grid.digits[level]
        return (self.grid.me() // (1 << low)) % size

    def copy(self, level, slot, k, arriving=False):
        low, size = self.grid.digits[level]
        rank = self.rank(level)
        to = (rank + k) % size
        buffer = self.buffers[level].at[slot]
        return pltpu.make_async_remote_copy(
            src_ref=buffer.at[rank],
            dst_ref=buffer.at[(rank + size - k) % size if arriving else rank],
            send_sem=self.send_sems[level].at[slot, k - 1],
            recv_sem=self.recv_sems[level].at[slot, k - 1],
            device_id=self.grid.place(self.grid.me() + (to - rank) * (1 << low)),
            device_id_type=MESH_ID,
        )

    def start(self, level, slot):
        for k in range(1, self.grid.digits[level][1]):
            self.copy(level, slot, k).start()

    def wait(self, level, slot):
        for k in range(1, self.grid.digits[level][1]):
            self.copy(level, slot, k, arriving=True).wait_recv()

    def finish(self, level, slot):
        for k in range(1, self.grid.digits[level][1]):
            self.copy(level, slot, k).wait_send()

    def own(self, level, slot):
        return self.buffers[level].at[slot, self.rank(level)]


def put_row(ref, first, row, width):
    full = width // 128
    for c in range(full):
        ref[first + c : first + c + 1, :] = row[:, 128 * c : 128 * (c + 1)]
    rest = width - 128 * full
    if rest:
        ref[first + full : first + full + 1, 0:rest] = row[:, 128 * full : width]


def take_row(block, first, width):
    pieces = []
    for c in range(-(-width // 128)):
        pieces.append(block[first + c : first + c + 1, 0 : min(128, width - 128 * c)])
    return jnp.concatenate(pieces, axis=1)


def row_loop(rows, body, init):
    steps = rows // ROWS

    def step(i, carry):
        return body(pl.ds(pl.multiple_of(i * ROWS, ROWS), ROWS), carry)

    return lax.fori_loop(0, steps, step, init)


def sigmoid(value):
    return 0.5 * jnp.tanh(0.5 * value) + 0.5


def column_sum(value):
    return jnp.sum(value, axis=0, keepdims=True)


PARTS = 32


def batch_norm(pre, nrm_out, act_out, gather, slot, gain_row, shift_row, inv_out, idle):
    rows, width = pre.shape
    total = row_loop(rows, lambda r, c: c + column_sum(pre[r, :]), jnp.zeros((1, width), F32))
    mean = total * (1.0 / rows)

    def squares(r, c):
        d = pre[r, :] - mean
        return c + column_sum(d * d)

    square = row_loop(rows, squares, jnp.zeros((1, width), F32))
    own = gather.own(0, slot)
    put_row(own, 0, mean, width)
    put_row(own, 8, square, width)
    count = float(rows)
    levels = len(gather.grid.digits)
    for level in range(levels):
        size = gather.grid.digits[level][1]
        gather.start(level, slot)
        idle(level)
        gather.wait(level, slot)
        buffer = gather.buffers[level].at[slot]
        means = [buffer[g, 0:8, :] for g in range(size)]
        merged = sum(means[1:], means[0]) * (1.0 / size)
        spread = sum([buffer[g, 8:16, :] for g in range(1, size)], buffer[0, 8:16, :])
        between = sum([(m - merged) * (m - merged) for m in means[1:]], (means[0] - merged) * (means[0] - merged))
        spread = spread + count * between
        count = count * size
        if level + 1 < levels:
            own = gather.own(level + 1, slot)
            own[0:8, :] = merged
            own[8:16, :] = spread
    inv = lax.rsqrt(spread * (1.0 / count) + NORM_EPSILON)
    mean = take_row(merged, 0, width)
    inv = take_row(inv, 0, width)
    inv_out[...] = inv

    def write(r, c):
        nrm = (pre[r, :] - mean) * inv
        nrm_out[r, :] = nrm
        value = gain_row * nrm + shift_row
        act_out[r, :] = (value * sigmoid(value)).astype(BF16)
        return c

    row_loop(rows, write, 0)


def nt(left, right):
    return lax.dot_general(left, right, (((1,), (1,)), ((), ())), preferred_element_type=F32)


def nn(left, right):
    return lax.dot_general(left, right, (((1,), (0,)), ((), ())), preferred_element_type=F32)


def tn(left, right):
    return lax.dot_general(left, right, (((0,), (0,)), ((), ())), preferred_element_type=F32)


def exact(left, right, dims):
    return lax.dot_general(
        left, right, (dims, ((), ())), precision=lax.Precision.HIGHEST, preferred_element_type=F32
    )


WIDE = 1024
AHEAD = 3


def windows(width, size=WIN):
    return [(s, min(size, width - s)) for s in range(0, width, size)]


def part_of(full, tail, i):
    return full.at[i] if i < full.shape[0] else tail


def forward_kernel(
    grid,
    table_ref,
    mask_ref,
    x_hbm,
    w1_hbm,
    noise_ref,
    gid_ref,
    w2_ref,
    head_ref,
    headb_ref,
    d1_ref,
    d2_ref,
    gain_ref,
    shift_ref,
    nrm0_hbm,
    nrm1_hbm,
    nrm2_hbm,
    nrm3_hbm,
    inv_out,
    act1_hbm,
    act2_hbm,
    zlat,
    act3_hbm,
    act4,
    head_out,
    ggroup_out,
    xt_out,
    offsets_out,
    x_all,
    xt,
    w_win,
    w_tail,
    pre,
    moments,
    *rest,
):
    levels = len(grid.digits)
    small = rest[:levels]
    wide = rest[levels : 2 * levels]
    s_send, s_recv, g_send, g_recv = (
        rest[2 * levels : 3 * levels],
        rest[3 * levels : 4 * levels],
        rest[4 * levels : 5 * levels],
        rest[5 * levels : 6 * levels],
    )
    in_sems, xt_sems, nrm_keep, act_keep, keep_sems = rest[6 * levels :]
    act1, act2, act3 = (act_keep.at[i] for i in range(3))
    gather = Gather(grid, small, s_send, s_recv)
    group_gather = Gather(grid, wide, g_send, g_recv)
    latent = d1_ref.shape[0]
    genes = x_hbm.shape[1]
    spans = windows(genes, WIDE)

    peers = digit_peers(grid)
    greet(grid, peers)
    loads = []
    for i, (s, size) in enumerate(spans):
        a = pltpu.make_async_copy(x_hbm.at[:, pl.ds(s, size)], x_all.at[:, pl.ds(s, size)], in_sems.at[0, i])
        b = pltpu.make_async_copy(w1_hbm.at[:, pl.ds(s, size)], part_of(w_win, w_tail, i), in_sems.at[1, i])
        if i < AHEAD:
            a.start()
            b.start()
        loads.append((a, b))

    for i, (s, size) in enumerate(spans):
        loads[i][0].wait()
        loads[i][1].wait()
        if i + AHEAD < len(loads):
            for copy in loads[i + AHEAD]:
                copy.start()
        part = nt(x_all[:, s : s + size], part_of(w_win, w_tail, i)[...])
        pre[...] = part if i == 0 else pre[...] + part

    starts = [(genes * j) // PARTS for j in range(PARTS)]
    parts_left = list(range(PARTS))

    def save(j):
        return pltpu.make_async_copy(xt.at[j], xt_out.at[j], xt_sems.at[j])

    def transpose(level):
        for j in parts_left[: -(-PARTS // 6)]:
            at = starts[j] // 128 * 128
            size = min(384, genes - at)
            lane = lax.broadcasted_iota(jnp.int32, (xt.shape[1], size), 1)
            line = lax.broadcasted_iota(jnp.int32, (xt.shape[1], size), 0)
            select = jnp.where(lane == line + (starts[j] - at), 1.0, 0.0).astype(BF16)
            xt[j] = nt(select, x_all[:, at : at + size]).astype(BF16)
            save(j).start()
            parts_left.remove(j)

    kept = [
        pltpu.make_async_copy(nrm_keep.at[k], ref, keep_sems.at[0, k])
        for k, ref in enumerate((nrm0_hbm, nrm1_hbm, nrm2_hbm, nrm3_hbm))
    ] + [
        pltpu.make_async_copy(act_keep.at[k], ref, keep_sems.at[1, k])
        for k, ref in enumerate((act1_hbm, act2_hbm, act3_hbm))
    ]

    def norm(k, act, idle=transpose):
        batch_norm(
            pre,
            nrm_keep.at[k],
            act,
            gather,
            k,
            gain_ref[k : k + 1, :],
            shift_ref[k : k + 1, :],
            inv_out.at[k : k + 1, :],
            idle,
        )
        kept[k].start()
        if k < 3:
            kept[4 + k].start()

    meet(peers)
    norm(0, act1)
    pre[...] = nn(act1[...], w2_ref[...])
    norm(1, act2)
    head = nt(act2[...], head_ref[...]) + headb_ref[...]
    head_out[...] = head
    mu = head[:, 0:latent]
    logvar = head[:, latent : 2 * latent]
    zlat[...] = (mu + jnp.exp(0.5 * logvar) * noise_ref[...].T).astype(BF16)

    groups = ggroup_out.shape[0]
    pops = groups // 2
    cells_here = gid_ref.shape[1]
    member = (lax.broadcasted_iota(jnp.int32, (groups, cells_here), 0) == gid_ref[...]).astype(F32)
    own = group_gather.own(0, 0)
    own[:, 0:latent] = exact(member, mu, ((1,), (0,)))
    own[:, latent : latent + 1] = jnp.sum(member, axis=1, keepdims=True)
    group_gather.start(0, 0)

    pre[...] = nn(zlat[...], d1_ref[...])
    norm(2, act3)

    def group_level(level):
        group_gather.wait(level, 0)
        size = grid.digits[level][1]
        buffer = wide[level].at[0]
        total = sum([buffer[g] for g in range(1, size)], buffer[0])
        if level + 1 < levels:
            group_gather.own(level + 1, 0)[...] = total
            group_gather.start(level + 1, 0)
            return
        counted = jnp.maximum(total[:, latent : latent + 1], 1.0)
        moments[...] = total / counted
        odd, even = pl.ds(1, pops, stride=2), pl.ds(0, pops, stride=2)
        offset = moments[odd, :] - moments[even, :]
        centre = jnp.sum(offset, axis=0, keepdims=True) * (1.0 / pops)
        grad_offset = (2.0 * OFFSET_WEIGHT / pops) * (offset - centre)
        row = lax.axis_index("cells")
        slots = offsets_out.shape[0]
        lane = lax.broadcasted_iota(jnp.int32, (1, pops), 1)
        picks = jnp.concatenate(
            [jnp.where(lane == table_ref[s, row], mask_ref[s, row].astype(F32), 0.0) for s in range(slots)], axis=0
        )
        offsets_out[...] = exact(picks, offset, ((1,), (0,)))[:, 0:latent]
        moments[odd, :] = grad_offset
        moments[even, :] = -grad_offset
        ggroup_out[...] = moments[...] / counted

    group_level(0)
    pre[...] = nn(act3[...], d2_ref[...])
    norm(3, act4, lambda level: group_level(level) if level else None)
    while parts_left:
        transpose(0)

    for j in range(PARTS):
        save(j).wait()
    for copy in kept:
        copy.wait()
    for level in range(levels):
        for k in range(4):
            gather.finish(level, k)
        group_gather.finish(level, 0)


XT_ROWS = 224


def call_forward(grid, cells_x, w1t, noise, gid, table, mask, w2, headt, headb, d1, d2, gain, shift):
    rows, genes = cells_x.shape
    hidden = w2.shape[0]
    latent = d1.shape[0]
    groups = 2 * POP_DEV * grid.cells
    spans = windows(genes, WIDE)
    count = len(spans)
    levels = len(grid.digits)
    vm = pl.BlockSpec(memory_space=pltpu.VMEM)
    hbm = pl.BlockSpec(memory_space=pl.ANY)
    sm = pl.BlockSpec(memory_space=pltpu.SMEM)
    wide_f = jax.ShapeDtypeStruct((rows, hidden), F32)
    wide_b = jax.ShapeDtypeStruct((rows, hidden), BF16)
    out_shape = (
        wide_f,
        wide_f,
        wide_f,
        wide_f,
        jax.ShapeDtypeStruct((4, hidden), F32),
        wide_b,
        wide_b,
        jax.ShapeDtypeStruct((rows, latent), BF16),
        wide_b,
        wide_b,
        jax.ShapeDtypeStruct((rows, 2 * latent), F32),
        jax.ShapeDtypeStruct((groups, 128), F32),
        jax.ShapeDtypeStruct((PARTS, XT_ROWS, rows), BF16),
        jax.ShapeDtypeStruct((table.shape[0], latent), F32),
    )
    scratch = (
        [
            pltpu.VMEM((rows, genes), BF16),
            pltpu.VMEM((PARTS, XT_ROWS, rows), BF16),
            pltpu.VMEM((count - 1, hidden, WIDE), BF16),
            pltpu.VMEM((hidden, spans[-1][1]), BF16),
            pltpu.VMEM((rows, hidden), F32),
            pltpu.VMEM((groups, 128), F32),
        ]
        + [pltpu.VMEM((4, size, 16, 128), F32) for _, size in grid.digits]
        + [pltpu.VMEM((1, size, groups, 128), F32) for _, size in grid.digits]
        + [pltpu.SemaphoreType.DMA((4, size - 1)) for _, size in grid.digits]
        + [pltpu.SemaphoreType.DMA((4, size - 1)) for _, size in grid.digits]
        + [pltpu.SemaphoreType.DMA((1, size - 1)) for _, size in grid.digits]
        + [pltpu.SemaphoreType.DMA((1, size - 1)) for _, size in grid.digits]
        + [pltpu.SemaphoreType.DMA((2, count)), pltpu.SemaphoreType.DMA((PARTS,))]
        + [
            pltpu.VMEM((4, rows, hidden), F32),
            pltpu.VMEM((3, rows, hidden), BF16),
            pltpu.SemaphoreType.DMA((2, 4)),
        ]
    )
    return pl.pallas_call(
        functools.partial(forward_kernel, grid),
        out_shape=out_shape,
        in_specs=[sm, sm, hbm, hbm] + [vm] * 9,
        out_specs=[hbm] * 4 + [vm, hbm, hbm, vm, hbm, vm, vm, vm, hbm, vm],
        scratch_shapes=scratch,
        name="forward",
        compiler_params=pltpu.CompilerParams(
            collective_id=0, has_side_effects=True, vmem_limit_bytes=60 * 2**20
        ),
    )(table, mask, cells_x, w1t, noise, gid, w2, headt, headb, d1, d2, gain, shift)


ORDERS = (
    (0, 2, 3, 1, 4),
    (0, 1, 3, 2, 4),
    (0, 2, 3, 1, 4),
    (0, 1, 3, 2, 4),
    (0, 2, 3, 1, 4),
    (0, 2, 3, 1, 4),
    (0, 1, 3, 2, 4),
    (0, 2, 3, 1, 4),
    (0, 1, 2, 3, 4),
    (0, 1, 3, 2, 4),
    (0, 2, 3, 1, 4),
    (0, 1, 2, 3, 4),
    (0, 1, 2, 3, 4),
    (0, 2, 3, 4, 1),
    (0, 2, 3, 1, 4),
    (0, 1, 2, 3, 4),
)
C, U, L, S, F, X, A = range(7)
PLAN = (
    (C,),
    (U, 0),
    (C,),
    (C,),
    (L, 0),
    (S, 0, 1, 7, 1),
    (S, 0, 1, 5, 2),
    (U, 1),
    (C,),
    (S, 0, 1, 4, 1),
    (C,),
    (L, 1),
    (S, 1, 1, 7, 1),
    (S, 0, 1, 3, 1),
    (C,),
    (S, 1, 1, 6, 1),
    (S, 0, 1, 2, 1),
    (C,),
    (F, 0, 1, 0),
    (S, 1, 1, 5, 1),
    (S, 0, 2, 3, 1),
    (S, 0, 1, 1, 1),
    (C,),
    (S, 1, 1, 4, 1),
    (S, 0, 1, 0, 1),
    (S, 0, 2, 2, 1),
    (C,),
    (S, 0, 2, 1, 1),
    (C,),
    (S, 1, 1, 3, 1),
    (S, 0, 2, 0, 1),
    (U, 2),
    (F, 0, 1, 1),
    (S, 1, 1, 2, 1),
    (F, 0, 2, 0),
    (F, 1, 1, 0),
    (S, 1, 2, 3, 1),
    (S, 1, 1, 1, 1),
    (C,),
    (S, 1, 2, 2, 1),
    (C,),
    (F, 0, 2, 1),
    (S, 1, 1, 0, 1),
    (L, 2),
    (S, 2, 1, 7, 1),
    (S, 0, 3, 1, 1),
    (S, 2, 1, 6, 1),
    (S, 1, 2, 1, 1),
    (U, 3),
    (S, 0, 3, 0, 1),
    (S, 1, 2, 0, 1),
    (C,),
    (F, 1, 1, 1),
    (S, 2, 1, 5, 1),
    (F, 1, 2, 0),
    (C,),
    (F, 0, 3, 0),
    (S, 2, 1, 4, 1),
    (S, 0, 4, 0, 1),
    (L, 3),
    (S, 3, 1, 7, 1),
    (F, 1, 2, 1),
    (C,),
    (C,),
    (S, 3, 1, 5, 2),
    (S, 2, 1, 2, 2),
    (F, 0, 3, 1),
    (U, 4),
    (F, 2, 1, 0),
    (S, 2, 2, 3, 1),
    (F, 0, 4, 0),
    (C,),
    (S, 3, 1, 4, 1),
    (S, 3, 1, 3, 1),
    (S, 2, 1, 0, 2),
    (S, 2, 2, 2, 1),
    (S, 2, 2, 1, 1),
    (L, 4),
    (U, 5),
    (F, 3, 1, 0),
    (S, 3, 1, 2, 1),
    (S, 1, 3, 1, 1),
    (S, 2, 2, 0, 1),
    (S, 3, 1, 1, 1),
    (S, 1, 3, 0, 1),
    (S, 3, 2, 3, 1),
    (C,),
    (F, 2, 1, 1),
    (F, 2, 2, 0),
    (L, 5),
    (S, 3, 1, 0, 1),
    (S, 4, 1, 7, 1),
    (S, 3, 2, 2, 1),
    (F, 1, 3, 0),
    (F, 2, 2, 1),
    (C,),
    (C,),
    (S, 2, 3, 1, 1),
    (S, 2, 3, 0, 1),
    (S, 4, 1, 5, 2),
    (S, 3, 2, 0, 2),
    (F, 1, 3, 1),
    (U, 6),
    (F, 3, 1, 1),
    (F, 3, 2, 0),
    (C,),
    (S, 4, 1, 4, 1),
    (S, 4, 1, 3, 1),
    (S, 1, 4, 0, 1),
    (F, 2, 3, 0),
    (F, 2, 3, 1),
    (L, 6),
    (S, 6, 1, 7, 1),
    (F, 3, 2, 1),
    (F, 4, 1, 0),
    (S, 6, 1, 6, 1),
    (S, 4, 1, 2, 1),
    (S, 2, 4, 0, 1),
    (S, 6, 1, 5, 1),
    (S, 4, 1, 1, 1),
    (C,),
    (F, 1, 4, 0),
    (C,),
    (C,),
    (S, 6, 1, 4, 1),
    (S, 6, 1, 3, 1),
    (S, 4, 1, 0, 1),
    (S, 3, 3, 1, 1),
    (S, 4, 2, 2, 2),
    (F, 2, 4, 0),
    (C,),
    (S, 6, 1, 1, 2),
    (S, 3, 3, 0, 1),
    (S, 5, 1, 7, 1),
    (S, 4, 2, 0, 2),
    (F, 4, 1, 1),
    (F, 6, 1, 0),
    (F, 3, 3, 0),
    (F, 4, 2, 0),
    (F, 3, 3, 1),
    (S, 6, 1, 0, 1),
    (S, 5, 1, 6, 1),
    (S, 3, 4, 0, 1),
    (S, 4, 3, 1, 1),
    (S, 5, 1, 5, 1),
    (C,),
    (F, 4, 2, 1),
    (C,),
    (C,),
    (S, 4, 3, 0, 1),
    (S, 5, 1, 4, 1),
    (S, 5, 1, 3, 1),
    (S, 6, 2, 2, 2),
    (F, 6, 1, 1),
    (F, 4, 3, 0),
    (A, 0),
    (F, 3, 4, 0),
    (A, 1),
    (C,),
    (S, 5, 1, 1, 2),
    (S, 6, 2, 0, 2),
    (F, 4, 3, 1),
    (F, 5, 1, 0),
    (F, 6, 2, 0),
    (S, 5, 1, 0, 1),
    (S, 6, 3, 1, 1),
    (S, 4, 4, 0, 1),
    (C,),
    (F, 6, 2, 1),
    (S, 6, 3, 0, 1),
    (S, 5, 2, 2, 2),
    (S, 5, 2, 0, 2),
    (A, 2),
    (U, 7),
    (F, 5, 1, 1),
    (X, 0),
    (F, 4, 4, 0),
    (F, 6, 3, 0),
    (S, 6, 4, 0, 1),
    (X, 1),
    (F, 6, 3, 1),
    (L, 7),
    (S, 7, 1, 4, 4),
    (S, 7, 1, 2, 2),
    (U, 8),
    (F, 5, 2, 0),
    (S, 5, 3, 1, 1),
    (S, 5, 3, 0, 1),
    (S, 7, 1, 1, 1),
    (A, 3),
    (X, 2),
    (X, 3),
    (L, 8),
    (S, 8, 1, 4, 4),
    (S, 8, 1, 1, 3),
    (S, 7, 1, 0, 1),
    (F, 5, 2, 1),
    (F, 5, 3, 0),
    (S, 5, 4, 0, 1),
    (U, 9),
    (F, 5, 3, 1),
    (S, 8, 1, 0, 1),
    (X, 4),
    (F, 6, 4, 0),
    (X, 5),
    (F, 7, 1, 0),
    (S, 7, 2, 2, 2),
    (S, 7, 2, 0, 2),
    (A, 4),
    (L, 9),
    (S, 9, 1, 6, 2),
    (U, 10),
    (F, 8, 1, 0),
    (S, 9, 1, 5, 1),
    (S, 9, 1, 4, 1),
    (S, 8, 2, 2, 2),
    (S, 8, 2, 0, 2),
    (X, 6),
    (F, 5, 4, 0),
    (X, 7),
    (X, 8),
    (L, 10),
    (S, 9, 1, 2, 2),
    (S, 10, 1, 4, 4),
    (F, 7, 1, 1),
    (X, 9),
    (F, 7, 2, 0),
    (S, 9, 1, 1, 1),
    (F, 8, 1, 1),
    (U, 11),
    (F, 8, 2, 0),
    (S, 9, 1, 0, 1),
    (S, 10, 1, 2, 2),
    (S, 8, 3, 1, 1),
    (S, 8, 3, 0, 1),
    (X, 10),
    (F, 7, 2, 1),
    (X, 11),
    (F, 8, 2, 1),
    (S, 7, 3, 1, 1),
    (S, 10, 1, 1, 1),
    (A, 5),
    (L, 11),
    (S, 7, 3, 0, 1),
    (F, 8, 3, 0),
    (S, 8, 4, 0, 1),
    (U, 12),
    (F, 8, 3, 1),
    (S, 11, 1, 7, 1),
    (S, 10, 1, 0, 1),
    (F, 9, 1, 0),
    (S, 9, 2, 2, 2),
    (S, 9, 2, 0, 2),
    (X, 12),
    (A, 6),
    (X, 13),
    (L, 12),
    (S, 11, 1, 6, 1),
    (F, 8, 4, 0),
    (F, 10, 1, 0),
    (S, 11, 1, 5, 1),
    (S, 10, 2, 2, 2),
    (S, 11, 1, 4, 1),
    (S, 10, 2, 0, 2),
    (F, 7, 3, 0),
    (S, 11, 1, 3, 1),
    (S, 11, 1, 2, 1),
    (S, 7, 4, 0, 1),
    (F, 9, 1, 1),
    (F, 9, 2, 0),
    (S, 9, 3, 1, 1),
    (S, 9, 3, 0, 1),
    (U, 13),
    (F, 7, 3, 1),
    (S, 11, 1, 1, 1),
    (F, 9, 2, 1),
    (F, 10, 1, 1),
    (A, 7),
    (S, 11, 1, 0, 1),
    (F, 9, 3, 0),
    (S, 9, 4, 0, 1),
    (F, 9, 3, 1),
    (S, 12, 1, 7, 1),
    (L, 13),
    (S, 13, 1, 4, 4),
    (S, 13, 1, 3, 1),
    (U, 14),
    (F, 10, 2, 0),
    (S, 12, 1, 6, 1),
    (S, 13, 1, 2, 1),
    (A, 8),
    (S, 13, 1, 1, 1),
    (F, 11, 1, 0),
    (F, 10, 2, 1),
    (S, 13, 1, 0, 1),
    (L, 14),
    (F, 7, 4, 0),
    (S, 11, 2, 2, 2),
    (F, 13, 1, 0),
    (S, 12, 1, 5, 1),
    (S, 11, 2, 1, 1),
    (S, 13, 2, 2, 2),
    (S, 13, 2, 0, 2),
    (F, 11, 1, 1),
    (S, 12, 1, 4, 1),
    (U, 15),
    (F, 9, 4, 0),
    (S, 12, 1, 3, 1),
    (S, 11, 2, 0, 1),
    (S, 14, 1, 7, 1),
    (S, 12, 1, 2, 1),
    (L, 15),
    (S, 12, 1, 1, 1),
    (S, 14, 1, 6, 1),
    (F, 13, 1, 1),
    (S, 14, 1, 5, 1),
    (F, 13, 2, 0),
    (S, 13, 3, 1, 1),
    (S, 13, 3, 0, 1),
    (F, 13, 2, 1),
    (S, 12, 1, 0, 1),
    (S, 14, 1, 4, 1),
    (A, 9),
    (S, 10, 3, 1, 1),
    (F, 11, 2, 0),
    (S, 14, 1, 3, 1),
    (S, 11, 3, 1, 1),
    (S, 11, 3, 0, 1),
    (A, 10),
    (S, 10, 3, 0, 1),
    (F, 13, 3, 0),
    (S, 14, 1, 2, 1),
    (F, 12, 1, 0),
    (S, 13, 4, 0, 1),
    (F, 11, 2, 1),
    (S, 14, 1, 1, 1),
    (S, 15, 1, 7, 1),
    (F, 13, 3, 1),
    (S, 14, 1, 0, 1),
    (F, 11, 3, 0),
    (S, 15, 1, 6, 1),
    (S, 12, 2, 3, 1),
    (S, 11, 4, 0, 1),
    (F, 11, 3, 1),
    (S, 15, 1, 5, 1),
    (S, 12, 2, 2, 1),
    (F, 12, 1, 1),
    (S, 15, 1, 4, 1),
    (F, 14, 1, 0),
    (S, 12, 2, 1, 1),
    (F, 10, 3, 0),
    (S, 10, 4, 0, 1),
    (S, 15, 1, 3, 1),
    (F, 11, 4, 0),
    (S, 12, 2, 0, 1),
    (F, 10, 3, 1),
    (S, 15, 1, 2, 1),
    (S, 14, 2, 2, 2),
    (S, 14, 2, 0, 2),
    (F, 13, 4, 0),
    (F, 10, 4, 0),
    (S, 15, 1, 1, 1),
    (F, 14, 1, 1),
    (S, 15, 1, 0, 1),
    (F, 14, 2, 0),
    (S, 14, 3, 1, 1),
    (F, 12, 2, 0),
    (S, 14, 3, 0, 1),
    (S, 12, 3, 1, 1),
    (S, 12, 3, 0, 1),
    (F, 15, 1, 0),
    (S, 15, 2, 2, 2),
    (S, 15, 2, 0, 2),
    (F, 14, 2, 1),
    (F, 12, 2, 1),
    (F, 12, 3, 0),
    (S, 12, 4, 0, 1),
    (F, 12, 3, 1),
    (F, 15, 1, 1),
    (F, 15, 2, 0),
    (S, 15, 3, 1, 1),
    (S, 15, 3, 0, 1),
    (F, 12, 4, 0),
    (F, 14, 3, 0),
    (S, 14, 4, 0, 1),
    (F, 15, 2, 1),
    (F, 15, 3, 0),
    (S, 15, 4, 0, 1),
    (F, 14, 3, 1),
    (F, 15, 3, 1),
    (F, 14, 4, 0),
    (F, 15, 4, 0),
)
CHANNELS = 4
STAGES = 5
SLOT_ROWS = 200


class Scatter:
    def __init__(self, grid, total, stage, low, landing, stage_sems, send_sems, recv_sems, credits):
        self.grid, self.total = grid, total
        self.stage, self.low, self.landing = stage, low, landing
        self.stage_sems, self.send_sems, self.recv_sems, self.credits = stage_sems, send_sems, recv_sems, credits
        self.shift = grid.bits - STAGES
        self.rows = {}

    def bit(self, b):
        return (self.grid.me() // (1 << (b + self.shift))) % 2

    def partner(self, b):
        return self.grid.place(self.grid.me() + (1 - 2 * self.bit(b)) * (1 << (b + self.shift)))

    def part(self, q, k):
        out = 0
        for t, b in enumerate(ORDERS[q]):
            own = self.bit(b)
            out = out + (1 << b) * ((1 - own) if (k >> (STAGES - 1 - t)) & 1 else own)
        return out

    def send(self, q, t, first=0, number=None):
        channel, rows = q % CHANNELS, self.rows[q]
        slots = 16 >> t
        at, size = first * rows, (slots if number is None else number) * rows
        if t == 0:
            source, sem = self.stage.at[q % 2, at : at + size], self.stage_sems.at[q % 2]
        else:
            start = slots * rows + at
            source, sem = self.landing[t - 1].at[channel, start : start + size], self.send_sems.at[channel, t]
        half = 0 if t == 0 or first >= slots // 2 else 1
        return pltpu.make_async_remote_copy(
            src_ref=source,
            dst_ref=self.landing[t].at[channel, at : at + size],
            send_sem=sem,
            recv_sem=self.recv_sems.at[channel, t, half],
            device_id=self.partner(ORDERS[q][t]),
            device_id_type=MESH_ID,
        )

    def feed(self, q, t, first, number):
        if first + number == 16 >> t and q >= CHANNELS:
            pl.semaphore_wait(self.credits.at[q - CHANNELS, t], 1)
        self.send(q, t, first, number).start()

    def free(self, q, t):
        if q + CHANNELS < self.total:
            pl.semaphore_signal(
                self.credits.at[q, t],
                inc=1,
                device_id=self.partner(ORDERS[q + CHANNELS][t]),
                device_id_type=MESH_ID,
            )

    def upper(self, q, rows, fill):
        self.rows[q] = rows
        if q >= 2:
            self.send(q - 2, 0).wait_send()
        fill(self.stage.at[q % 2], True)
        self.feed(q, 0, 0, 16)
        fill(self.low, False)

    def lower(self, q):
        channel, rows = q % CHANNELS, self.rows[q]
        self.send(q, 0).wait_recv()
        mine = self.landing[0].at[channel]

        def add(i, c):
            r = pl.ds(pl.multiple_of(i * rows, 8), rows)
            mine[r, :] += self.low[r, :]
            return c

        lax.fori_loop(0, 16, add, 0)

    def fold(self, q, t, half):
        channel, rows = q % CHANNELS, self.rows[q]
        number = 8 >> t
        first = number if half == 0 else 0
        self.send(q, t, first, number).wait_recv()
        mine, before = self.landing[t].at[channel], self.landing[t - 1].at[channel]

        def add(i, c):
            r = pl.ds(pl.multiple_of(i * rows, 8), rows)
            mine[r, :] += before[r, :]
            return c

        lax.fori_loop(first, first + number, add, 0)
        if half == 1:
            self.send(q, t).wait_send()
            self.free(q, t - 1)

    def last(self, q, done):
        channel, rows = q % CHANNELS, self.rows[q]
        t = STAGES - 1
        self.send(q, t).wait_recv()
        done(self.landing[t][channel, 0:rows, :] + self.landing[t - 1][channel, 0:rows, :])
        self.send(q, t).wait_send()
        self.free(q, t - 1)
        self.free(q, t)


class Spread:
    def __init__(self, scatter, block, landing, whole, sems):
        self.scatter, self.block, self.landing, self.whole, self.sems = scatter, block, landing, whole, sems
        self.rows = block.shape[0]

    def begin(self, t):
        out = 0
        for i in range(t):
            out = out + self.scatter.bit(i) * (self.rows >> (i + 1))
        return out

    def halving(self, t):
        size = self.rows >> (t + 1)
        at = self.begin(t) + (1 - self.scatter.bit(t)) * size
        return pltpu.make_async_remote_copy(
            src_ref=self.block.at[pl.ds(pl.multiple_of(at, 8), size)],
            dst_ref=self.landing[t],
            send_sem=self.sems.at[0, t],
            recv_sem=self.sems.at[1, t],
            device_id=self.scatter.partner(t),
            device_id_type=MESH_ID,
        )

    def doubling(self, t, arriving=False):
        size = self.rows >> (t + 1)
        at = self.begin(t + 1)
        there = self.begin(t) + (1 - self.scatter.bit(t)) * size if arriving else at
        return pltpu.make_async_remote_copy(
            src_ref=self.whole.at[pl.ds(pl.multiple_of(at, 8), size)],
            dst_ref=self.whole.at[pl.ds(pl.multiple_of(there, 8), size)],
            send_sem=self.sems.at[2, t],
            recv_sem=self.sems.at[3, t],
            device_id=self.scatter.partner(t),
            device_id_type=MESH_ID,
        )

    def step(self, i):
        if i == 0:
            self.halving(0).start()
        elif i <= STAGES:
            t = i - 1
            self.halving(t).wait_recv()
            size = self.rows >> (t + 1)
            r = pl.ds(pl.multiple_of(self.begin(t + 1), 8), size)
            target = self.whole if i == STAGES else self.block
            target[r, :] = self.block[r, :] + self.landing[t][...]
            self.halving(t).wait_send()
            if i < STAGES:
                self.halving(t + 1).start()
            else:
                self.doubling(t).start()
        else:
            t = 2 * STAGES - i
            self.doubling(t, True).wait_recv()
            self.doubling(t).wait_send()
            if t > 0:
                self.doubling(t - 1).start()


def one_hot(rows, target):
    lane = lax.broadcasted_iota(jnp.int32, (rows, target.shape[1]), 0)
    return jnp.where(lane == target, 1.0, 0.0).astype(BF16)


def column_parts(width, size):
    column = lax.broadcasted_iota(jnp.int32, (1, width), 1)
    part = jnp.zeros((1, width), jnp.int32)
    for m in range(1, width // size):
        part = part + jnp.where(column >= m * size, 1, 0)
    return column, part


def slot_of(scatter, q, bits, parts, part):
    order = [b for b in ORDERS[q] if b in bits]
    slot = jnp.zeros_like(part)
    for value in range(parts):
        at = 0
        for t, b in enumerate(order):
            own = scatter.bit(b)
            weight = 1 << (len(order) - 1 - t)
            at = at + weight * ((1 - own) if (value >> bits.index(b)) & 1 else own)
        slot = jnp.where(part == value, at, slot)
    return slot


def sum_blocks(gather, slot):
    levels = len(gather.grid.digits)
    yield
    for level in range(levels):
        gather.start(level, slot)
        if level < 2:
            yield
        gather.wait(level, slot)
        size = gather.grid.digits[level][1]
        buffer = gather.buffers[level].at[slot]
        total = sum([buffer[g] for g in range(1, size)], buffer[0])
        if level + 1 < levels:
            gather.own(level + 1, slot)[...] = total
    return total


def norm_gradient(grad, nrm, out, gather, slot, gain_row, shift_row, inv_row, scale, gain_out, shift_out):
    rows, width = grad.shape

    def gate(r, carry):
        n = nrm[r, :]
        value = gain_row * n + shift_row
        sig = sigmoid(value)
        g = grad[r, :] * sig * (1.0 + value * (1.0 - sig))
        grad[r, :] = g
        return carry[0] + column_sum(g), carry[1] + column_sum(g * n)

    zero = jnp.zeros((1, width), F32)
    shift_sum, gain_sum = row_loop(rows, gate, (zero, zero))
    own = gather.own(0, slot)
    put_row(own, 0, shift_sum, width)
    put_row(own, 8, gain_sum, width)
    total = yield from sum_blocks(gather, slot)
    shift_sum = take_row(total, 0, width)
    gain_sum = take_row(total, 8, width)
    shift_out[...] = shift_sum
    gain_out[...] = gain_sum
    factor = gain_row * inv_row
    shift_mean = shift_sum * scale
    gain_mean = gain_sum * scale

    def write(r, c):
        out[r, :] = (factor * (grad[r, :] - shift_mean - nrm[r, :] * gain_mean)).astype(BF16)
        return c

    row_loop(rows, write, 0)


D1_ROWS = 104
GX = 512
REP_ROWS = 2304


def backward_kernel(
    grid,
    latent,
    x_hbm,
    w1_hbm,
    outw_hbm,
    nrm_hbm0,
    nrm_hbm1,
    nrm_hbm2,
    nrm_hbm3,
    act1_hbm,
    act2_hbm,
    act3_hbm,
    xt_hbm,
    act4_ref,
    zlat_ref,
    head_ref_in,
    noise_ref,
    gid_ref,
    ggroup_ref,
    inv_ref,
    outb_ref,
    w2_ref,
    head_ref,
    d1_ref,
    d2_ref,
    gain_ref,
    shift_ref,
    g_out,
    gx_out,
    out25,
    enc_part,
    nar_part,
    d1_out,
    headw_out,
    outb_out,
    headb_out,
    gain_out,
    shift_out,
    *rest,
):
    levels = len(grid.digits)
    rest = list(rest)

    def take(n):
        got = rest[:n]
        del rest[:n]
        return got

    small, s_send, s_recv = take(levels), take(levels), take(levels)
    stage, low, *landing = take(2 + STAGES)
    stage_sems, send_sems, recv_sems, credits = take(4)
    rep_block, rep_whole, *rep_landing = take(2 + STAGES)
    (rep_sems,) = take(1)
    g_win, wide, gact, gpre4, gpre3, gpre2, gpre1, ghead, gcell, lhs, nrm_buf, fin = take(12)
    distinct = sorted(set(ORDERS[: -(-x_hbm.shape[1] // WIN)]))
    lhs_at = [distinct.index(o) if o in distinct else None for o in ORDERS]
    picked = lhs.at[0, 0:512]
    in_sems, g_sems, nrm_sems, xt_sem, act_sems, gx_sems = take(6)

    rows, genes = x_hbm.shape
    hidden = w2_ref.shape[0]
    spans = windows(genes)
    count = len(spans)
    cell_total = float(rows * grid.n)
    total = 2 * count + 2
    gather = Gather(grid, small, s_send, s_recv)
    first = count
    scatter = Scatter(grid, total, stage, low, landing, stage_sems, send_sems, recv_sems, credits)
    spread = Spread(scatter, rep_block, rep_landing, rep_whole, rep_sems)
    rep_outb = 7 * (D1_ROWS + 2 * latent)
    rep_headb = rep_outb + 8 * count

    peers = digit_peers(grid)
    greet(grid, peers)
    nrm_loads = {
        k: pltpu.make_async_copy(ref, nrm_buf.at[(k + 1) % 2], nrm_sems.at[k])
        for k, ref in enumerate((nrm_hbm0, nrm_hbm1, nrm_hbm2, nrm_hbm3))
    }
    nrm_loads[3].start()
    nrm_loads[2].start()


    def out_fill(s):
        buffer = g_win.at[s % 3]

        def fill(target, is_upper):
            first = hidden // 2 if is_upper else 0
            part = nn(lhs[lhs_at[s], first : first + hidden // 2, :], buffer[...])
            for c in range(WIN // 128):
                target[pl.ds(c, hidden // 2, stride=8), :] = part[:, 128 * c : 128 * (c + 1)]

        return fill

    def out_lhs(q):
        if ORDERS[q] in ORDERS[:q]:
            return
        mine = lhs.at[lhs_at[q]]
        column, part = column_parts(hidden, hidden // PARTS)
        slot = slot_of(scatter, q, (0, 1, 2, 3, 4), PARTS, part)
        target = column + (hidden // PARTS) * (slot - part)
        block = hidden // 5

        def some(i, c):
            at = pl.multiple_of(i * block, block)
            mine[pl.ds(at, block), :] = nt(one_hot(block, target - at), act4_ref[...]).astype(BF16)
            return c

        lax.fori_loop(0, 5, some, 0)

    def out_done(s):
        def done(value):
            fin[...] = value
            for c in range(WIN // 128):
                out25[:, WIN * s + 128 * c : WIN * s + 128 * (c + 1)] = fin[pl.ds(c, hidden // PARTS, stride=8), :]

        return done

    done = {s: out_done(s) for s in range(count)}
    pieces = {}
    for s in range(count):
        pieces[s] = (SLOT_ROWS, out_fill(s))

    plan = list(PLAN)

    def run(chain, cells=None):
        while plan:
            what, *which = plan[0]
            if what == C:
                if next(chain, None) is None:
                    return
            elif what == U:
                if which[0] < count:
                    out_lhs(which[0])
                scatter.upper(which[0], *pieces[which[0]])
            elif what == L:
                scatter.lower(which[0])
            elif what == S:
                scatter.feed(*which)
            elif what == X:
                cells(*which)
            elif what == A:
                spread.step(*which)
            elif which[1] < STAGES - 1:
                scatter.fold(*which)
            else:
                scatter.last(which[0], done[which[0]])
            del plan[0]

    def output_layer(w_ring, w_tail, x_ring, x_tail):
        def load(s):
            at, size = spans[s]
            tail = s == count - 1
            return (
                pltpu.make_async_copy(
                    outw_hbm.at[:, pl.ds(at, size)], w_tail if tail else w_ring.at[s % 3], in_sems.at[0, s]
                ),
                pltpu.make_async_copy(
                    x_hbm.at[:, pl.ds(at, size)], x_tail if tail else x_ring.at[s % 2], in_sems.at[1, s]
                ),
            )

        def save(s):
            return pltpu.make_async_copy(g_win.at[s % 3], g_out.at[:, pl.ds(WIN * s, WIN)], g_sems.at[s])

        def layers():
            for s in range(2):
                for copy in load(s):
                    copy.start()
            for s in range(count):
                yield from layer(s)

        def layer(s):
            at, size = spans[s]
            tail = s == count - 1
            w = w_tail if tail else w_ring.at[s % 3]
            x = x_tail if tail else x_ring.at[s % 2]
            for copy in load(s):
                copy.wait()
            wide[:, 0:size] = nn(act4_ref[...], w[...])
            bias = outb_ref[:, at : at + size]
            if s >= 3:
                save(s - 3).wait()
            g = g_win.at[s % 3]

            def residual(r, c):
                value = wide[r, 0:size] + bias - x[r, :].astype(F32)
                value = (value * (2.0 / cell_total)).astype(BF16)
                g[r, 0:size] = value
                return c + column_sum(value.astype(F32))

            put_row(rep_block, rep_outb + 8 * s, row_loop(rows, residual, jnp.zeros((1, size), F32)), size)
            if size < WIN:
                g[:, size:WIN] = jnp.zeros((rows, WIN - size), BF16)
            save(s).start()
            if s == 0:
                meet(peers)
            if s + 2 < count:
                for copy in load(s + 2):
                    copy.start()
            yield 0
            part = nt(g[:, 0:size], w[...])
            gact[...] = part if s == 0 else gact[...] + part
            yield 0

        run(layers())
        for s in range(count - 3, count):
            save(s).wait()

    pl.run_scoped(
        output_layer,
        pltpu.VMEM((3, hidden, WIN), BF16),
        pltpu.VMEM((hidden, spans[-1][1]), BF16),
        pltpu.VMEM((2, rows, WIN), BF16),
        pltpu.VMEM((rows, spans[-1][1]), BF16),
    )


    def pack(target, at, source, row, height):
        full = hidden // 128
        for c in range(full):
            target[pl.ds(pl.multiple_of(at + height * c, 8), height), :] = source[
                pl.ds(row, height), 128 * c : 128 * (c + 1)
            ]
        rest_width = hidden - 128 * full
        pieces = [source[pl.ds(row + 8 * i, 8), 128 * full : hidden] for i in range(height // 8)]
        target[pl.ds(pl.multiple_of(at + height * full, 8), 8), 0 : rest_width * len(pieces)] = jnp.concatenate(
            pieces, axis=1
        )

    def unpack(value, out, row, height):
        full = hidden // 128
        rest_width = hidden - 128 * full
        for c in range(full):
            out[row : row + height, 128 * c : 128 * (c + 1)] = value[height * c : height * (c + 1), :]
        for i in range(height // 8):
            out[row + 8 * i : row + 8 * i + 8, 128 * full : hidden] = value[
                height * full : height * full + 8, rest_width * i : rest_width * (i + 1)
            ]

    def finish(xt, act_buf, w1_ring, w1_tail, gx_ring):
        xt_load = pltpu.make_async_copy(xt_hbm, xt, xt_sem)
        xt_load.start()

        gx_spans = windows(genes, GX)

        def gx_load(i):
            at, size = gx_spans[i]
            return (
                pltpu.make_async_copy(
                    w1_hbm.at[:, pl.ds(at, size)], w1_ring.at[i % 2] if size == GX else w1_tail, gx_sems.at[0, i]
                ),
                pltpu.make_async_copy(
                    g_out.at[:, pl.ds(at, GX)], g_win.at[i % 2, :, pl.ds(0, GX)], gx_sems.at[1, i]
                ),
            )

        def gx_save(i):
            return pltpu.make_async_copy(gx_ring.at[i % 2], gx_out.at[:, pl.ds(GX * i, GX)], gx_sems.at[2, i])

        def grad_cells(i):
            at, size = gx_spans[i]
            if i == 0:
                for copy in gx_load(0):
                    copy.start()
            if i + 1 < len(gx_spans):
                for copy in gx_load(i + 1):
                    copy.start()
            for copy in gx_load(i):
                copy.wait()
            if i >= 2:
                gx_save(i - 2).wait()
            wide[:, 0:size] = nn(gpre1[...], w1_ring[i % 2] if size == GX else w1_tail[...])

            def write(r, c):
                value = wide[r, 0:size] - g_win[i % 2, r, 0:size].astype(F32)
                gx_ring[i % 2, r, 0:size] = (cell_total * value).astype(BF16)
                return c

            row_loop(rows, write, 0)
            gx_save(i).start()
            if i + 1 == len(gx_spans):
                gx_save(i - 1).wait()
                gx_save(i).wait()

        def enc_fill(q, s):
            def fill(target, is_upper):
                for i in range(16):
                    j = scatter.part(q, 16 + i if is_upper else i)
                    picked[32 * i : 32 * i + 32, :] = xt[j, 32 * s : 32 * s + 32, :]
                wide[0:512, 0:hidden] = nn(picked[...], gpre1[...])

                def one(i, c):
                    pack(target, i * SLOT_ROWS, wide, pl.multiple_of(i * 32, 32), 32)
                    return c

                lax.fori_loop(0, 16, one, 0)

            return fill

        def enc_done(s):
            return lambda value: unpack(value, enc_part, 32 * s, 32)

        each = 2 * hidden // PARTS
        skip = (0, 32)

        def nar_fill(q, which):
            height_here = 32 if which == 0 else 24
            rows_here = 25 * 8 if which == 0 else 19 * 8
            place = STAGES - 1 - ORDERS[q].index(4)

            def fill(target, is_upper):
                column, part = column_parts(hidden, each)
                slot = slot_of(scatter, q, (0, 1, 2, 3), PARTS // 2, part)
                line = column - each * part - skip[which]
                inside = (line >= 0) & (line < height_here)
                base = 8 if is_upper else 0
                place_in = jnp.where(inside, (slot - base) * height_here + line, -1)
                place_in = jnp.where((slot >= base) & (slot < base + 8), place_in, -1)
                select = one_hot(8 * height_here, place_in)
                for matrix, act_slot, grad in ((0, 0, gpre2), (1, 1, gpre4)):
                    size = 8 * height_here
                    picked[0:size, :] = nt(select, act_buf[act_slot]).astype(BF16)
                    wide[0:size, 0:hidden] = nn(picked[0:size, :], grad[...])
                    flip = scatter.bit(4) if matrix == 0 else 1 - scatter.bit(4)
                    for i in range(8):
                        k = (i >> place) * (2 << place) + (i & ((1 << place) - 1)) + flip * (1 << place)
                        pack(target, k * rows_here, wide, i * height_here, height_here)

            return rows_here, fill

        def nar_done(which):
            if which == 0:
                return lambda value: unpack(value, nar_part, 0, 32)
            return lambda value: unpack(value, nar_part, 32, 24)

        for which in range(2):
            done[first + which] = nar_done(which)
            pieces[first + which] = nar_fill(first + which, which)
        for s in range(count):
            done[first + 2 + s] = enc_done(s)
            pieces[first + 2 + s] = (SLOT_ROWS, enc_fill(first + 2 + s, s))

        def row(ref, k):
            return ref[k : k + 1, :]

        def back(k, grad, out):
            nrm_loads[k].wait()
            return norm_gradient(
                grad,
                nrm_buf.at[(k + 1) % 2],
                out,
                gather,
                k,
                row(gain_ref, k),
                row(shift_ref, k),
                row(inv_ref, k),
                1.0 / cell_total,
                gain_out.at[k : k + 1, :],
                shift_out.at[k : k + 1, :],
            )

        act_loads = [
            pltpu.make_async_copy(ref, act_buf.at[at], act_sems.at[i])
            for i, (ref, at) in enumerate(((act1_hbm, 0), (act3_hbm, 1), (act2_hbm, 0)))
        ]
        act_loads[1].start()
        act_loads[2].start()

        def latent_side():
            act_loads[2].wait()
            d1_grad = tn(zlat_ref[...], gpre3[...])
            headw_grad = tn(ghead[...], act_buf[0])
            act_loads[0].start()
            for c in range(-(-hidden // 128)):
                size = min(128, hidden - 128 * c)
                at = D1_ROWS * c
                rep_block[at : at + latent, 0:size] = d1_grad[:, 128 * c : 128 * c + size]
                at = 7 * D1_ROWS + 2 * latent * c
                rep_block[at : at + 2 * latent, 0:size] = headw_grad[:, 128 * c : 128 * c + size]
            put_row(rep_block, rep_headb, column_sum(ghead[...].astype(F32)), 2 * latent)

        def chain():
            for k, out in ((3, gpre4), (2, gpre3), (1, gpre2), (0, gpre1)):
                waits = back(k, gact, out)
                for at, _ in enumerate(waits):
                    if (k, at) == (3, 1):
                        groups = ggroup_ref.shape[0]
                        member = (lax.broadcasted_iota(jnp.int32, (groups, rows), 0) == gid_ref[...]).astype(F32)
                        gcell[...] = exact(member, ggroup_ref[...], ((0,), (0,)))
                    if (k, at) == (1, 1):
                        latent_side()
                    yield 0
                if k == 3:
                    nrm_loads[1].start()
                    gact[...] = nt(gpre4[...], d2_ref[...])
                elif k == 2:
                    nrm_loads[0].start()
                    grad_z = nt(gpre3[...], d1_ref[...])
                    mu = head_ref_in[:, 0:latent]
                    logvar = head_ref_in[:, latent : 2 * latent]
                    kl = KL_WEIGHT * genes / cell_total
                    deviation = jnp.exp(0.5 * logvar)
                    grad_mu = grad_z + kl * mu + gcell[:, 0:latent]
                    grad_logvar = grad_z * noise_ref[...].T * (0.5 * deviation) + 0.5 * kl * (jnp.exp(logvar) - 1.0)
                    ghead[...] = jnp.concatenate([grad_mu, grad_logvar], axis=1).astype(BF16)
                    gact[...] = nn(ghead[...], head_ref[...])
                elif k == 1:
                    gact[...] = nt(gpre2[...], w2_ref[...])
                else:
                    for copy in act_loads[:2]:
                        copy.wait()
                    xt_load.wait()
                yield 0

        run(chain(), grad_cells)
        for q in (total - 2, total - 1):
            scatter.send(q, 0).wait_send()
        for c in range(-(-hidden // 128)):
            size = min(128, hidden - 128 * c)
            at = D1_ROWS * c
            d1_out[:, 128 * c : 128 * c + size] = rep_whole[at : at + latent, 0:size]
            at = 7 * D1_ROWS + 2 * latent * c
            headw_out[:, 128 * c : 128 * c + size] = rep_whole[at : at + 2 * latent, 0:size]
        outb_out[...] = rep_whole[rep_outb : rep_outb + 8 * count, :]
        headb_out[...] = rep_whole[rep_headb : rep_headb + 8, :]
        for level in range(levels):
            for k in range(4):
                gather.finish(level, k)

    pl.run_scoped(
        finish,
        pltpu.VMEM(xt_hbm.shape, BF16),
        pltpu.VMEM((2, rows, hidden), BF16),
        pltpu.VMEM((2, hidden, GX), BF16),
        pltpu.VMEM((hidden, windows(genes, GX)[-1][1]), BF16),
        pltpu.VMEM((2, rows, GX), BF16),
    )


def call_backward(grid, kept, cells_x, w1t, out_w, noise, gid, out_b, w2, headt, d1, d2, gain, shift):
    (nrm0, nrm1, nrm2, nrm3, inv, act1, act2, zlat, act3, act4, head, ggroup, xt) = kept
    rows, genes = cells_x.shape
    hidden, latent = w2.shape[0], d1.shape[0]
    spans = windows(genes)
    count = len(spans)
    vm = pl.BlockSpec(memory_space=pltpu.VMEM)
    hbm = pl.BlockSpec(memory_space=pl.ANY)
    shape = jax.ShapeDtypeStruct
    out_shape = (
        shape((rows, WIN * count), BF16),
        shape((rows, WIN * count), BF16),
        shape((hidden // PARTS, WIN * count), F32),
        shape((32 * count, hidden), F32),
        shape((56, hidden), F32),
        shape((latent, hidden), F32),
        shape((2 * latent, hidden), F32),
        shape((8 * count, 128), F32),
        shape((8, 128), F32),
        shape((4, hidden), F32),
        shape((4, hidden), F32),
    )
    dma = pltpu.SemaphoreType.DMA
    scratch = (
        [pltpu.VMEM((4, size, 16, 128), F32) for _, size in grid.digits]
        + [dma((4, size - 1)) for _, size in grid.digits]
        + [dma((4, size - 1)) for _, size in grid.digits]
        + [pltpu.VMEM((2, 16 * SLOT_ROWS, 128), F32), pltpu.VMEM((16 * SLOT_ROWS, 128), F32)]
        + [pltpu.VMEM((CHANNELS, (16 >> t) * SLOT_ROWS, 128), F32) for t in range(STAGES)]
        + [dma((2,)), dma((CHANNELS, STAGES)), dma((CHANNELS, STAGES, 2)), pltpu.SemaphoreType.REGULAR((2 * count + 2 - CHANNELS, STAGES))]
        + [pltpu.VMEM((REP_ROWS, 128), F32), pltpu.VMEM((REP_ROWS, 128), F32)]
        + [pltpu.VMEM((REP_ROWS >> (t + 1), 128), F32) for t in range(STAGES)]
        + [dma((4, STAGES))]
        + [
            pltpu.VMEM((3, rows, WIN), BF16),
            pltpu.VMEM((rows, WIN), F32),
            pltpu.VMEM((rows, hidden), F32),
            pltpu.VMEM((rows, hidden), BF16),
            pltpu.VMEM((rows, hidden), BF16),
            pltpu.VMEM((rows, hidden), BF16),
            pltpu.VMEM((rows, hidden), BF16),
            pltpu.VMEM((rows, 2 * latent), BF16),
            pltpu.VMEM((rows, 128), F32),
            pltpu.VMEM((len(set(ORDERS[:count])), hidden, rows), BF16),
            pltpu.VMEM((2, rows, hidden), F32),
            pltpu.VMEM((SLOT_ROWS, 128), F32),
        ]
        + [dma((2, count)), dma((count,)), dma((4,)), dma, dma((3,)), dma((3, len(windows(genes, GX))))]
    )
    return pl.pallas_call(
        functools.partial(backward_kernel, grid, latent),
        out_shape=out_shape,
        in_specs=[hbm] * 11 + [vm] * 14,
        out_specs=[hbm] * 2 + [vm] * (len(out_shape) - 2),
        scratch_shapes=scratch,
        name="backward",
        compiler_params=pltpu.CompilerParams(
            collective_id=1, has_side_effects=True, vmem_limit_bytes=63 * 2**20
        ),
    )(
        cells_x,
        w1t,
        out_w,
        nrm0,
        nrm1,
        nrm2,
        nrm3,
        act1,
        act2,
        act3,
        xt,
        act4,
        zlat,
        head,
        noise,
        gid,
        ggroup,
        inv,
        out_b,
        w2,
        headt,
        d1,
        d2,
        gain,
        shift,
    )


def flat_shard(grid, flat, columns, rows_in_all):
    value = flat.reshape(rows_in_all // PARTS, columns)
    size = grid.n // PARTS
    if size > 1:
        groups = [list(range(size * p, size * p + size)) for p in range(PARTS)]
        value = lax.psum_scatter(
            value, ("cells", "rep"), scatter_dimension=0, axis_index_groups=groups, tiled=True
        )
    return value


def group_sum(grid, values):
    size = grid.n // PARTS
    if size > 1:
        groups = [list(range(size * p, size * p + size)) for p in range(PARTS)]
        values = lax.psum(values, ("cells", "rep"), axis_index_groups=groups)
    return values


def shards(
    grid,
    cells_x,
    latent_noise,
    group_ids,
    owner_table,
    owner_mask,
    enc_w1,
    enc_w2,
    head_w,
    head_b,
    dec_w1,
    dec_w2,
    out_w,
    out_b,
    bn_gain,
    bn_shift,
):
    cell_total = float(cells_x.shape[0] * grid.n)
    genes = cells_x.shape[1]
    hidden = enc_w2.shape[0]
    gid = group_ids.reshape(1, -1)
    headt = head_w.T
    w1t = enc_w1.T
    noise = latent_noise.T
    *kept, offsets = call_forward(
        grid,
        cells_x,
        w1t,
        noise,
        gid,
        owner_table.T,
        owner_mask.T,
        enc_w2,
        headt,
        head_b.reshape(1, -1),
        dec_w1,
        dec_w2,
        bn_gain,
        bn_shift,
    )
    _, gx, out25, enc_part, nar_part, d1_grad, headw_grad, outb_grad, headb_grad, grad_gain, grad_shift = call_backward(
        grid,
        kept,
        cells_x,
        w1t,
        out_w,
        noise,
        gid,
        out_b.reshape(1, -1),
        enc_w2,
        headt,
        dec_w1,
        dec_w2,
        bn_gain,
        bn_shift,
    )
    grad_x = gx[:, :genes].astype(F32)
    part = grid.me() // (grid.n // PARTS)
    each = genes * hidden // PARTS
    enc_flat = lax.dynamic_slice_in_dim(enc_part.reshape(-1), (genes * part) % PARTS * (hidden // PARTS), each)
    shard_enc = flat_shard(grid, enc_flat, FLAT_COLS, FLAT_ROWS)
    shard_out = flat_shard(grid, out25[:, :genes], FLAT_COLS, FLAT_ROWS)
    shard_narrow = flat_shard(grid, nar_part[: 2 * hidden // PARTS], NARROW_COLS, NARROW_ROWS)
    headw_grad, d1_grad, headb_grad, outb_grad = group_sum(
        grid,
        (headw_grad.T, d1_grad, headb_grad.reshape(-1)[: head_b.shape[0]], outb_grad.reshape(-1)[:genes]),
    )
    return (
        grad_x,
        shard_enc,
        shard_narrow,
        headw_grad,
        d1_grad,
        headb_grad,
        shard_out,
        outb_grad,
        grad_gain,
        grad_shift,
        offsets[None],
    )


def solution(mesh):
    grid = Slice(mesh.shape["cells"], mesh.shape["rep"])
    lines = P(("cells", "rep"), None)
    return jax.shard_map(
        functools.partial(shards, grid),
        mesh=mesh,
        in_specs=(lines, lines, P(("cells", "rep"))) + (P(),) * 12,
        out_specs=(lines, lines, lines, P(), P(), P(), lines, P(), P(), P(), P("cells", None, None)),
        check_vma=False,
    )
```

profile of v0, /device:TPU:0, one launch (start us, length us, event | category | flops | bytes accessed | tf_op | source)
XLA Modules:
  0.0 328.0 jit_solution(5281422550547145684)
XLA Ops:
  0.6 1.3 reshape.49.gid_ref
  1.9 0.0 copy-start.4
  1.9 58.7 %forward.1 = (f32[576,800]{1,0:T(8,128)}, f32[576,800]{1,0:T(8,128)}, f32[576,800]{1,0:T(8,128)}, f32[576,800]{1,0:T(8,128)}, f32[4,800]{1,0:T(4,128)}, /*index=...) custom-call(s32[4,16]{1,0:T(4,128)} %bitcast.21, ...), custom_call_target="tpu_custom_call" | custom-call | tf_op jit(solution)/shard_map/forward/pallas_call | solution.py:450
  60.7 0.0 copy-done.4
  60.7 0.6 reshape.51.outb_ref
  61.3 244.8 %backward.1 = (bf16[576,7168]{1,0:T(8,128)(2,1)}, bf16[576,7168]{1,0:T(8,128)(2,1)}, f32[25,7168]{1,0:T(8,128)}, f32[224,800]{1,0:T(8,128)}, f32[56,800]{1,0:T(8...) custom-call(bf16[576,7000]{1,0:T(8,128)(2,1)} %x_hbm.3, ...), custom_call_target="tpu_custom_call" | custom-call | tf_op jit(solution)/shard_map/backward/pallas_call | solution.py:1609
  306.1 0.0 copy-start.1
  306.1 0.0 copy-start
  306.1 10.6 %slice_convert_fusion = f32[576,7000]{1,0:T(8,128)} fusion(bf16[576,7168]{1,0:T(8,128)(2,1)} %get-tuple-element.48), kind=kLoop, calls=%fused_computation | loop fusion | flops 4032000 | bytes 24192000 | tf_op jit(solution)/shard_map/convert_element_type | solution.py:1724
  316.7 0.0 copy-start.2
  316.7 0.0 copy-start.3
  316.7 0.0 copy-start.5
  316.7 0.0 copy-done.1
  316.7 0.6 reshape.52
  317.3 0.0 copy-start.7
  317.3 0.0 copy-start.6
  317.3 0.0 copy-start.8
  317.3 0.3 dynamic_slice.3
  317.6 1.5 reshape.53
  319.1 0.0 copy-done
  319.1 0.1 slice.18
  319.2 1.3 reshape.56
  320.5 1.8 reshape.54
  322.3 1.2 slice.17
  323.5 0.0 copy-done.2
  323.5 0.9 copy.32
  324.4 0.0 copy-done.3
  324.4 0.7 copy.33
  325.1 0.0 copy-done.5
  325.1 0.6 copy.34
  325.7 0.0 copy-done.7
  325.7 0.6 copy.35
  326.3 0.0 copy-done.6
  326.3 0.6 copy.36
  326.9 0.0 copy-done.8
  326.9 0.6 copy.37
Async XLA Ops:
  1.9 58.8 %copy-start.4 = (f32[7000]{0:T(1024)S(1)}, f32[7000]{0:T(1024)}, u32[]{:S(2)}) copy-start(f32[7000]{0:T(1024)} %param.27) | copy-start | bytes 84004
  306.1 10.6 %copy-start.1 = (f32[224,800]{1,0:T(8,128)S(1)}, f32[224,800]{1,0:T(8,128)}, u32[]{:S(2)}) copy-start(f32[224,800]{1,0:T(8,128)} %get-tuple-element.49) | copy-start | bytes 2150404
  306.1 13.0 %copy-start = (f32[25,7168]{1,0:T(8,128)S(1)}, f32[25,7168]{1,0:T(8,128)}, u32[]{:S(2)}) copy-start(f32[25,7168]{1,0:T(8,128)} %get-tuple-element.54) | copy-start | bytes 2150404
  316.7 6.8 %copy-start.2 = (f32[200,800]{1,0:T(8,128)S(1)}, f32[200,800]{1,0:T(8,128)}, u32[]{:S(2)}) copy-start(f32[200,800]{1,0:T(8,128)} %get-tuple-element.51) | copy-start | bytes 1920004
  316.7 7.7 %copy-start.3 = (f32[100,800]{1,0:T(8,128)S(1)}, f32[100,800]{1,0:T(8,128)}, u32[]{:S(2)}) copy-start(f32[100,800]{1,0:T(8,128)} %get-tuple-element.74) | copy-start | bytes 960004
  316.7 8.4 %copy-start.5 = (f32[56,128]{1,0:T(8,128)S(1)}, f32[56,128]{1,0:T(8,128)}, u32[]{:S(2)}) copy-start(f32[56,128]{1,0:T(8,128)} %get-tuple-element.55) | copy-start | bytes 86020
  317.3 8.4 %copy-start.7 = (f32[4,800]{1,0:T(4,128)S(1)}, f32[4,800]{1,0:T(4,128)}, u32[]{:S(2)}) copy-start(f32[4,800]{1,0:T(4,128)} %get-tuple-element.78) | copy-start | bytes 38404
  317.3 9.0 %copy-start.6 = (f32[4,800]{1,0:T(4,128)S(1)}, f32[4,800]{1,0:T(4,128)}, u32[]{:S(2)}) copy-start(f32[4,800]{1,0:T(4,128)} %get-tuple-element.79) | copy-start | bytes 38404
  317.3 9.6 %copy-start.8 = (f32[4,100]{1,0:T(4,128)S(1)}, f32[4,100]{1,0:T(4,128)}, u32[]{:S(2)}) copy-start(f32[4,100]{1,0:T(4,128)} %get-tuple-element.58) | copy-start | bytes 4804
where the time goes:
time: 334 us; the launch traced here: 328 us
  Pallas kernels  304 us (91%)
  local copies, waits for them, and re-layouts  12.7 us (4%)
  other arithmetic  10.6 us (3%)
    pallas_call x1, Pallas kernels, call_backward(): pl.pallas_call(functools.partial(backward_kernel, grid, latent), out_shap...  245 us
    pallas_call x1, Pallas kernels, call_forward(): pl.pallas_call(functools.partial(forward_kernel, grid), out_shape=out_sha...  58.7 us
    convert_element_type x1, other arithmetic, shards(): grad_x = gx[:, :genes].astype(F32)  10.6 us

commit v1 on v0

--- a/solution.py
+++ b/solution.py
@@ -461,20 +461,20 @@
 
 
 ORDERS = (
-    (0, 2, 3, 1, 4),
     (0, 1, 3, 2, 4),
-    (0, 2, 3, 1, 4),
+    (0, 2, 1, 3, 4),
     (0, 1, 3, 2, 4),
-    (0, 2, 3, 1, 4),
-    (0, 2, 3, 1, 4),
+    (0, 2, 1, 3, 4),
+    (0, 2, 1, 3, 4),
     (0, 1, 3, 2, 4),
-    (0, 2, 3, 1, 4),
+    (0, 2, 1, 3, 4),
+    (0, 1, 3, 2, 4),
+    (0, 2, 1, 3, 4),
+    (0, 2, 1, 3, 4),
     (0, 1, 2, 3, 4),
+    (0, 3, 2, 1, 4),
+    (0, 2, 1, 3, 4),
     (0, 1, 3, 2, 4),
-    (0, 2, 3, 1, 4),
-    (0, 1, 2, 3, 4),
-    (0, 1, 2, 3, 4),
-    (0, 2, 3, 4, 1),
     (0, 2, 3, 1, 4),
     (0, 1, 2, 3, 4),
 )
@@ -488,384 +488,378 @@
     (S, 0, 1, 7, 1),
     (S, 0, 1, 5, 2),
     (U, 1),
-    (C,),
     (S, 0, 1, 4, 1),
+    (C,),
+    (S, 0, 1, 3, 1),
     (C,),
     (L, 1),
     (S, 1, 1, 7, 1),
-    (S, 0, 1, 3, 1),
-    (C,),
+    (S, 0, 1, 2, 1),
     (S, 1, 1, 6, 1),
-    (S, 0, 1, 2, 1),
+    (C,),
+    (S, 0, 1, 1, 1),
+    (S, 1, 1, 5, 1),
     (C,),
     (F, 0, 1, 0),
-    (S, 1, 1, 5, 1),
     (S, 0, 2, 3, 1),
-    (S, 0, 1, 1, 1),
-    (C,),
+    (S, 0, 1, 0, 1),
     (S, 1, 1, 4, 1),
-    (S, 0, 1, 0, 1),
     (S, 0, 2, 2, 1),
     (C,),
+    (S, 1, 1, 3, 1),
     (S, 0, 2, 1, 1),
     (C,),
-    (S, 1, 1, 3, 1),
     (S, 0, 2, 0, 1),
+    (C,),
+    (S, 1, 1, 2, 1),
     (U, 2),
     (F, 0, 1, 1),
-    (S, 1, 1, 2, 1),
     (F, 0, 2, 0),
     (F, 1, 1, 0),
     (S, 1, 2, 3, 1),
-    (S, 1, 1, 1, 1),
-    (C,),
     (S, 1, 2, 2, 1),
+    (S, 1, 1, 0, 2),
+    (C,),
+    (S, 1, 2, 1, 1),
     (C,),
     (F, 0, 2, 1),
-    (S, 1, 1, 0, 1),
     (L, 2),
+    (S, 1, 2, 0, 1),
+    (S, 0, 3, 1, 1),
+    (S, 0, 3, 0, 1),
+    (U, 3),
     (S, 2, 1, 7, 1),
-    (S, 0, 3, 1, 1),
+    (C,),
+    (F, 1, 1, 1),
+    (F, 1, 2, 0),
+    (S, 1, 3, 1, 1),
     (S, 2, 1, 6, 1),
-    (S, 1, 2, 1, 1),
-    (U, 3),
-    (S, 0, 3, 0, 1),
-    (S, 1, 2, 0, 1),
-    (C,),
-    (F, 1, 1, 1),
-    (S, 2, 1, 5, 1),
-    (F, 1, 2, 0),
+    (S, 1, 3, 0, 1),
     (C,),
     (F, 0, 3, 0),
-    (S, 2, 1, 4, 1),
-    (S, 0, 4, 0, 1),
+    (F, 1, 2, 1),
     (L, 3),
     (S, 3, 1, 7, 1),
-    (F, 1, 2, 1),
-    (C,),
-    (C,),
-    (S, 3, 1, 5, 2),
+    (C,),
+    (C,),
+    (S, 2, 1, 4, 2),
     (S, 2, 1, 2, 2),
+    (S, 3, 1, 4, 3),
+    (S, 3, 1, 3, 1),
+    (S, 0, 4, 0, 1),
     (F, 0, 3, 1),
+    (F, 1, 3, 0),
     (U, 4),
+    (F, 1, 3, 1),
+    (C,),
+    (S, 2, 1, 1, 1),
+    (S, 3, 1, 2, 1),
+    (S, 1, 4, 0, 1),
     (F, 2, 1, 0),
+    (F, 0, 4, 0),
+    (L, 4),
     (S, 2, 2, 3, 1),
-    (F, 0, 4, 0),
-    (C,),
-    (S, 3, 1, 4, 1),
-    (S, 3, 1, 3, 1),
-    (S, 2, 1, 0, 2),
+    (U, 5),
+    (F, 3, 1, 0),
+    (S, 2, 1, 0, 1),
+    (S, 3, 2, 3, 1),
+    (S, 3, 1, 0, 2),
     (S, 2, 2, 2, 1),
     (S, 2, 2, 1, 1),
-    (L, 4),
-    (U, 5),
-    (F, 3, 1, 0),
-    (S, 3, 1, 2, 1),
-    (S, 1, 3, 1, 1),
+    (C,),
+    (F, 1, 4, 0),
+    (L, 5),
+    (C,),
+    (C,),
+    (S, 3, 2, 2, 1),
+    (S, 3, 2, 0, 2),
+    (S, 5, 1, 7, 1),
+    (S, 4, 1, 4, 4),
     (S, 2, 2, 0, 1),
-    (S, 3, 1, 1, 1),
-    (S, 1, 3, 0, 1),
-    (S, 3, 2, 3, 1),
-    (C,),
     (F, 2, 1, 1),
     (F, 2, 2, 0),
-    (L, 5),
-    (S, 3, 1, 0, 1),
-    (S, 4, 1, 7, 1),
-    (S, 3, 2, 2, 1),
-    (F, 1, 3, 0),
+    (F, 3, 1, 1),
+    (U, 6),
+    (C,),
+    (S, 5, 1, 5, 2),
+    (S, 4, 1, 3, 1),
+    (S, 4, 1, 2, 1),
     (F, 2, 2, 1),
-    (C,),
-    (C,),
+    (F, 3, 2, 0),
+    (S, 3, 3, 1, 1),
+    (S, 3, 3, 0, 1),
+    (L, 6),
+    (C,),
+    (F, 3, 2, 1),
+    (F, 3, 3, 0),
+    (S, 3, 4, 0, 1),
+    (F, 3, 3, 1),
+    (F, 4, 1, 0),
+    (C,),
+    (C,),
+    (S, 5, 1, 4, 1),
+    (S, 5, 1, 1, 3),
+    (S, 4, 1, 0, 2),
     (S, 2, 3, 1, 1),
     (S, 2, 3, 0, 1),
-    (S, 4, 1, 5, 2),
-    (S, 3, 2, 0, 2),
-    (F, 1, 3, 1),
-    (U, 6),
-    (F, 3, 1, 1),
-    (F, 3, 2, 0),
-    (C,),
-    (S, 4, 1, 4, 1),
-    (S, 4, 1, 3, 1),
-    (S, 1, 4, 0, 1),
+    (F, 3, 4, 0),
+    (C,),
+    (S, 5, 1, 0, 1),
+    (S, 6, 1, 7, 1),
+    (F, 5, 1, 0),
+    (S, 5, 2, 3, 1),
+    (F, 4, 1, 1),
+    (S, 5, 2, 2, 1),
+    (S, 4, 2, 3, 1),
+    (S, 6, 1, 6, 1),
+    (S, 5, 2, 0, 2),
+    (C,),
     (F, 2, 3, 0),
     (F, 2, 3, 1),
-    (L, 6),
-    (S, 6, 1, 7, 1),
-    (F, 3, 2, 1),
-    (F, 4, 1, 0),
-    (S, 6, 1, 6, 1),
-    (S, 4, 1, 2, 1),
+    (C,),
+    (C,),
+    (S, 4, 2, 2, 1),
+    (S, 4, 2, 0, 2),
+    (S, 6, 1, 4, 2),
+    (S, 6, 1, 2, 2),
     (S, 2, 4, 0, 1),
-    (S, 6, 1, 5, 1),
-    (S, 4, 1, 1, 1),
-    (C,),
-    (F, 1, 4, 0),
-    (C,),
-    (C,),
-    (S, 6, 1, 4, 1),
-    (S, 6, 1, 3, 1),
-    (S, 4, 1, 0, 1),
-    (S, 3, 3, 1, 1),
-    (S, 4, 2, 2, 2),
+    (F, 5, 1, 1),
+    (F, 5, 2, 0),
+    (A, 0),
+    (F, 5, 2, 1),
+    (A, 1),
+    (C,),
+    (S, 6, 1, 1, 1),
+    (F, 4, 2, 0),
+    (S, 4, 3, 1, 1),
+    (F, 6, 1, 0),
+    (S, 4, 3, 0, 1),
     (F, 2, 4, 0),
-    (C,),
-    (S, 6, 1, 1, 2),
-    (S, 3, 3, 0, 1),
-    (S, 5, 1, 7, 1),
-    (S, 4, 2, 0, 2),
-    (F, 4, 1, 1),
-    (F, 6, 1, 0),
-    (F, 3, 3, 0),
-    (F, 4, 2, 0),
-    (F, 3, 3, 1),
+    (F, 4, 2, 1),
+    (F, 4, 3, 0),
+    (S, 4, 4, 0, 1),
+    (S, 6, 2, 3, 1),
     (S, 6, 1, 0, 1),
-    (S, 5, 1, 6, 1),
-    (S, 3, 4, 0, 1),
-    (S, 4, 3, 1, 1),
-    (S, 5, 1, 5, 1),
-    (C,),
-    (F, 4, 2, 1),
-    (C,),
-    (C,),
-    (S, 4, 3, 0, 1),
-    (S, 5, 1, 4, 1),
-    (S, 5, 1, 3, 1),
-    (S, 6, 2, 2, 2),
-    (F, 6, 1, 1),
-    (F, 4, 3, 0),
-    (A, 0),
-    (F, 3, 4, 0),
-    (A, 1),
-    (C,),
-    (S, 5, 1, 1, 2),
+    (S, 5, 3, 1, 1),
+    (C,),
+    (F, 4, 3, 1),
+    (S, 6, 2, 2, 1),
     (S, 6, 2, 0, 2),
-    (F, 4, 3, 1),
-    (F, 5, 1, 0),
-    (F, 6, 2, 0),
-    (S, 5, 1, 0, 1),
-    (S, 6, 3, 1, 1),
-    (S, 4, 4, 0, 1),
-    (C,),
-    (F, 6, 2, 1),
-    (S, 6, 3, 0, 1),
-    (S, 5, 2, 2, 2),
-    (S, 5, 2, 0, 2),
-    (A, 2),
+    (S, 5, 3, 0, 1),
     (U, 7),
-    (F, 5, 1, 1),
     (X, 0),
     (F, 4, 4, 0),
-    (F, 6, 3, 0),
-    (S, 6, 4, 0, 1),
+    (F, 6, 1, 1),
+    (A, 2),
     (X, 1),
-    (F, 6, 3, 1),
+    (F, 5, 3, 0),
+    (S, 5, 4, 0, 1),
     (L, 7),
     (S, 7, 1, 4, 4),
-    (S, 7, 1, 2, 2),
     (U, 8),
-    (F, 5, 2, 0),
-    (S, 5, 3, 1, 1),
-    (S, 5, 3, 0, 1),
-    (S, 7, 1, 1, 1),
-    (A, 3),
+    (F, 5, 3, 1),
+    (S, 7, 1, 3, 1),
+    (F, 6, 2, 0),
+    (S, 6, 3, 1, 1),
+    (S, 6, 3, 0, 1),
     (X, 2),
     (X, 3),
+    (F, 5, 4, 0),
+    (S, 7, 1, 1, 2),
+    (F, 6, 2, 1),
+    (A, 3),
     (L, 8),
     (S, 8, 1, 4, 4),
-    (S, 8, 1, 1, 3),
+    (S, 8, 1, 0, 4),
+    (U, 9),
+    (F, 6, 3, 0),
     (S, 7, 1, 0, 1),
-    (F, 5, 2, 1),
-    (F, 5, 3, 0),
-    (S, 5, 4, 0, 1),
-    (U, 9),
-    (F, 5, 3, 1),
-    (S, 8, 1, 0, 1),
+    (S, 6, 4, 0, 1),
     (X, 4),
-    (F, 6, 4, 0),
+    (F, 6, 3, 1),
     (X, 5),
-    (F, 7, 1, 0),
-    (S, 7, 2, 2, 2),
-    (S, 7, 2, 0, 2),
     (A, 4),
     (L, 9),
     (S, 9, 1, 6, 2),
+    (S, 9, 1, 5, 1),
     (U, 10),
+    (F, 7, 1, 0),
+    (S, 9, 1, 4, 1),
+    (S, 7, 2, 2, 2),
+    (S, 7, 2, 0, 2),
     (F, 8, 1, 0),
-    (S, 9, 1, 5, 1),
-    (S, 9, 1, 4, 1),
     (S, 8, 2, 2, 2),
     (S, 8, 2, 0, 2),
     (X, 6),
-    (F, 5, 4, 0),
+    (F, 6, 4, 0),
+    (S, 9, 1, 3, 1),
     (X, 7),
+    (A, 5),
+    (L, 10),
+    (S, 10, 1, 6, 2),
     (X, 8),
-    (L, 10),
-    (S, 9, 1, 2, 2),
-    (S, 10, 1, 4, 4),
+    (X, 9),
+    (F, 8, 1, 1),
+    (S, 10, 1, 5, 1),
+    (S, 9, 1, 1, 2),
+    (X, 10),
     (F, 7, 1, 1),
-    (X, 9),
+    (S, 10, 1, 4, 1),
+    (S, 9, 1, 0, 1),
     (F, 7, 2, 0),
-    (S, 9, 1, 1, 1),
-    (F, 8, 1, 1),
+    (X, 11),
     (U, 11),
+    (F, 7, 2, 1),
+    (S, 10, 1, 2, 2),
+    (S, 7, 3, 1, 1),
     (F, 8, 2, 0),
-    (S, 9, 1, 0, 1),
-    (S, 10, 1, 2, 2),
     (S, 8, 3, 1, 1),
     (S, 8, 3, 0, 1),
-    (X, 10),
-    (F, 7, 2, 1),
-    (X, 11),
+    (A, 6),
+    (X, 12),
     (F, 8, 2, 1),
-    (S, 7, 3, 1, 1),
     (S, 10, 1, 1, 1),
-    (A, 5),
-    (L, 11),
     (S, 7, 3, 0, 1),
+    (X, 13),
     (F, 8, 3, 0),
     (S, 8, 4, 0, 1),
+    (F, 9, 1, 0),
+    (L, 11),
+    (S, 10, 1, 0, 1),
+    (S, 11, 1, 4, 4),
     (U, 12),
     (F, 8, 3, 1),
-    (S, 11, 1, 7, 1),
-    (S, 10, 1, 0, 1),
-    (F, 9, 1, 0),
-    (S, 9, 2, 2, 2),
-    (S, 9, 2, 0, 2),
-    (X, 12),
-    (A, 6),
-    (X, 13),
+    (S, 9, 2, 3, 1),
+    (S, 11, 1, 3, 1),
+    (A, 7),
+    (S, 9, 2, 2, 1),
+    (S, 11, 1, 2, 1),
+    (F, 8, 4, 0),
     (L, 12),
-    (S, 11, 1, 6, 1),
-    (F, 8, 4, 0),
+    (S, 12, 1, 5, 3),
+    (S, 11, 1, 1, 1),
     (F, 10, 1, 0),
-    (S, 11, 1, 5, 1),
-    (S, 10, 2, 2, 2),
-    (S, 11, 1, 4, 1),
-    (S, 10, 2, 0, 2),
+    (S, 9, 2, 1, 1),
+    (F, 9, 1, 1),
+    (U, 13),
     (F, 7, 3, 0),
-    (S, 11, 1, 3, 1),
-    (S, 11, 1, 2, 1),
+    (S, 9, 2, 0, 1),
+    (S, 12, 1, 4, 1),
+    (S, 12, 1, 3, 1),
+    (S, 11, 1, 0, 1),
     (S, 7, 4, 0, 1),
-    (F, 9, 1, 1),
+    (F, 7, 3, 1),
+    (S, 12, 1, 2, 1),
+    (L, 13),
+    (F, 11, 1, 0),
+    (S, 12, 1, 1, 1),
+    (A, 8),
+    (F, 10, 1, 1),
+    (U, 14),
+    (S, 12, 1, 0, 1),
     (F, 9, 2, 0),
+    (S, 10, 2, 3, 1),
     (S, 9, 3, 1, 1),
     (S, 9, 3, 0, 1),
-    (U, 13),
-    (F, 7, 3, 1),
-    (S, 11, 1, 1, 1),
+    (L, 14),
+    (S, 10, 2, 2, 1),
+    (F, 11, 1, 1),
+    (S, 10, 2, 1, 1),
+    (F, 12, 1, 0),
+    (S, 12, 2, 2, 2),
+    (S, 12, 2, 1, 1),
     (F, 9, 2, 1),
-    (F, 10, 1, 1),
-    (A, 7),
-    (S, 11, 1, 0, 1),
+    (S, 12, 2, 0, 1),
+    (U, 15),
+    (S, 13, 1, 7, 1),
+    (S, 10, 2, 0, 1),
+    (F, 7, 4, 0),
+    (S, 13, 1, 6, 1),
+    (S, 11, 2, 3, 1),
     (F, 9, 3, 0),
     (S, 9, 4, 0, 1),
+    (L, 15),
+    (S, 11, 2, 2, 1),
+    (A, 9),
+    (S, 13, 1, 5, 1),
     (F, 9, 3, 1),
-    (S, 12, 1, 7, 1),
-    (L, 13),
-    (S, 13, 1, 4, 4),
+    (F, 12, 1, 1),
+    (S, 11, 2, 1, 1),
+    (A, 10),
+    (S, 13, 1, 4, 1),
+    (F, 12, 2, 0),
     (S, 13, 1, 3, 1),
-    (U, 14),
+    (S, 11, 2, 0, 1),
+    (S, 12, 3, 1, 1),
+    (S, 12, 3, 0, 1),
+    (F, 9, 4, 0),
     (F, 10, 2, 0),
-    (S, 12, 1, 6, 1),
+    (S, 10, 3, 1, 1),
+    (S, 10, 3, 0, 1),
     (S, 13, 1, 2, 1),
-    (A, 8),
+    (F, 12, 2, 1),
     (S, 13, 1, 1, 1),
-    (F, 11, 1, 0),
+    (F, 12, 3, 0),
+    (S, 12, 4, 0, 1),
+    (F, 12, 3, 1),
     (F, 10, 2, 1),
     (S, 13, 1, 0, 1),
-    (L, 14),
-    (F, 7, 4, 0),
-    (S, 11, 2, 2, 2),
+    (S, 14, 1, 5, 3),
+    (F, 10, 3, 0),
+    (S, 10, 4, 0, 1),
+    (F, 10, 3, 1),
+    (S, 14, 1, 4, 1),
+    (F, 11, 2, 0),
+    (S, 11, 3, 1, 1),
+    (S, 14, 1, 3, 1),
     (F, 13, 1, 0),
-    (S, 12, 1, 5, 1),
-    (S, 11, 2, 1, 1),
+    (S, 11, 3, 0, 1),
+    (S, 14, 1, 2, 1),
     (S, 13, 2, 2, 2),
     (S, 13, 2, 0, 2),
-    (F, 11, 1, 1),
-    (S, 12, 1, 4, 1),
-    (U, 15),
-    (F, 9, 4, 0),
-    (S, 12, 1, 3, 1),
-    (S, 11, 2, 0, 1),
-    (S, 14, 1, 7, 1),
-    (S, 12, 1, 2, 1),
-    (L, 15),
-    (S, 12, 1, 1, 1),
-    (S, 14, 1, 6, 1),
+    (F, 12, 4, 0),
+    (F, 11, 2, 1),
+    (S, 14, 1, 1, 1),
+    (S, 15, 1, 6, 2),
+    (F, 10, 4, 0),
+    (S, 15, 1, 5, 1),
+    (S, 14, 1, 0, 1),
     (F, 13, 1, 1),
-    (S, 14, 1, 5, 1),
+    (S, 15, 1, 4, 1),
+    (S, 15, 1, 3, 1),
     (F, 13, 2, 0),
     (S, 13, 3, 1, 1),
     (S, 13, 3, 0, 1),
-    (F, 13, 2, 1),
-    (S, 12, 1, 0, 1),
-    (S, 14, 1, 4, 1),
-    (A, 9),
-    (S, 10, 3, 1, 1),
-    (F, 11, 2, 0),
-    (S, 14, 1, 3, 1),
-    (S, 11, 3, 1, 1),
-    (S, 11, 3, 0, 1),
-    (A, 10),
-    (S, 10, 3, 0, 1),
-    (F, 13, 3, 0),
-    (S, 14, 1, 2, 1),
-    (F, 12, 1, 0),
-    (S, 13, 4, 0, 1),
-    (F, 11, 2, 1),
-    (S, 14, 1, 1, 1),
-    (S, 15, 1, 7, 1),
-    (F, 13, 3, 1),
-    (S, 14, 1, 0, 1),
+    (F, 14, 1, 0),
+    (S, 14, 2, 2, 2),
+    (S, 14, 2, 0, 2),
     (F, 11, 3, 0),
-    (S, 15, 1, 6, 1),
-    (S, 12, 2, 3, 1),
+    (S, 15, 1, 2, 1),
     (S, 11, 4, 0, 1),
     (F, 11, 3, 1),
-    (S, 15, 1, 5, 1),
-    (S, 12, 2, 2, 1),
-    (F, 12, 1, 1),
-    (S, 15, 1, 4, 1),
-    (F, 14, 1, 0),
-    (S, 12, 2, 1, 1),
-    (F, 10, 3, 0),
-    (S, 10, 4, 0, 1),
-    (S, 15, 1, 3, 1),
-    (F, 11, 4, 0),
-    (S, 12, 2, 0, 1),
-    (F, 10, 3, 1),
-    (S, 15, 1, 2, 1),
-    (S, 14, 2, 2, 2),
-    (S, 14, 2, 0, 2),
-    (F, 13, 4, 0),
-    (F, 10, 4, 0),
+    (F, 13, 2, 1),
     (S, 15, 1, 1, 1),
+    (S, 15, 1, 0, 1),
+    (F, 13, 3, 0),
+    (S, 13, 4, 0, 1),
     (F, 14, 1, 1),
-    (S, 15, 1, 0, 1),
     (F, 14, 2, 0),
     (S, 14, 3, 1, 1),
-    (F, 12, 2, 0),
     (S, 14, 3, 0, 1),
-    (S, 12, 3, 1, 1),
-    (S, 12, 3, 0, 1),
     (F, 15, 1, 0),
     (S, 15, 2, 2, 2),
     (S, 15, 2, 0, 2),
     (F, 14, 2, 1),
-    (F, 12, 2, 1),
-    (F, 12, 3, 0),
-    (S, 12, 4, 0, 1),
-    (F, 12, 3, 1),
+    (F, 13, 3, 1),
+    (F, 11, 4, 0),
     (F, 15, 1, 1),
     (F, 15, 2, 0),
     (S, 15, 3, 1, 1),
     (S, 15, 3, 0, 1),
-    (F, 12, 4, 0),
+    (F, 13, 4, 0),
+    (F, 15, 2, 1),
     (F, 14, 3, 0),
     (S, 14, 4, 0, 1),
-    (F, 15, 2, 1),
     (F, 15, 3, 0),
     (S, 15, 4, 0, 1),
     (F, 14, 3, 1),
@@ -1645,6 +1639,25 @@
     )
 
 
+def widen(value, width):
+    rows = value.shape[0]
+    block = 96
+
+    def kernel(a, b):
+        b[...] = a[:, 0:width].astype(F32)
+
+    return pl.pallas_call(
+        kernel,
+        out_shape=jax.ShapeDtypeStruct((rows, width), F32),
+        grid=(rows // block,),
+        in_specs=[pl.BlockSpec((block, value.shape[1]), lambda i: (i, 0))],
+        out_specs=pl.BlockSpec((block, width), lambda i: (i, 0)),
+        name="widen",
+        cost_estimate=pl.CostEstimate(flops=0, bytes_accessed=6 * rows * width, transcendentals=0),
+        compiler_params=pltpu.CompilerParams(vmem_limit_bytes=62 * 2**20),
+    )(value)
+
+
 def flat_shard(grid, flat, columns, rows_in_all):
     value = flat.reshape(rows_in_all // PARTS, columns)
     size = grid.n // PARTS
@@ -1721,7 +1734,7 @@
         bn_gain,
         bn_shift,
     )
-    grad_x = gx[:, :genes].astype(F32)
+    grad_x = widen(gx, genes)
     part = grid.me() // (grid.n // PARTS)
     each = genes * hidden // PARTS
     enc_flat = lax.dynamic_slice_in_dim(enc_part.reshape(-1), (genes * part) % PARTS * (hidden // PARTS), each)

time: 334 us -> 327 us (0.979)
  other arithmetic: 10.6 us -> 0 us
    convert_element_type x1 -> x0, other arithmetic: 10.6 us -> none  [shards(): grad_x = gx[:, :genes].astype(F32)]
    pallas_call x0 -> x1, Pallas kernels: none -> 9.98 us  [widen(): pl.pallas_call(kernel, out_shape=jax.ShapeDtypeStruct((rows, width), F32)...]
    pallas_call x1, Pallas kernels: 245 us -> 238 us  [call_backward(): pl.pallas_call(functools.partial(backward_kernel, grid, latent), out_shap...]
where the time goes in v1:
time: 327 us; the launch traced here: 321 us
  Pallas kernels  307 us (94%)
  local copies, waits for them, and re-layouts  12.9 us (4%)
    pallas_call x1, Pallas kernels, call_backward(): pl.pallas_call(functools.partial(backward_kernel, grid, latent), out_shap...  238 us
    pallas_call x1, Pallas kernels, call_forward(): pl.pallas_call(functools.partial(forward_kernel, grid), out_shape=out_sha...  58.7 us
    pallas_call x1, Pallas kernels, widen(): pl.pallas_call(kernel, out_shape=jax.ShapeDtypeStruct((rows, width), F32)...  9.98 us

profile of v1, /device:TPU:0, one launch (start us, length us, event | category | flops | bytes accessed | tf_op | source)
XLA Modules:
  0.0 321.0 jit_solution(2480422736212857681)
XLA Ops:
  0.6 1.3 reshape.49.gid_ref
  1.9 0.0 copy-start.4
  1.9 58.7 %forward.1 = (f32[576,800]{1,0:T(8,128)}, f32[576,800]{1,0:T(8,128)}, f32[576,800]{1,0:T(8,128)}, f32[576,800]{1,0:T(8,128)}, f32[4,800]{1,0:T(4,128)}, /*index=...) custom-call(s32[4,16]{1,0:T(4,128)} %bitcast.21, ...), custom_call_target="tpu_custom_call" | custom-call | tf_op jit(solution)/shard_map/forward/pallas_call | solution.py:450
  60.7 0.0 copy-done.4
  60.7 0.6 reshape.51.outb_ref
  61.3 238.1 %backward.1 = (bf16[576,7168]{1,0:T(8,128)(2,1)}, bf16[576,7168]{1,0:T(8,128)(2,1)}, f32[25,7168]{1,0:T(8,128)}, f32[224,800]{1,0:T(8,128)}, f32[56,800]{1,0:T(8...) custom-call(bf16[576,7000]{1,0:T(8,128)(2,1)} %x_hbm.3, ...), custom_call_target="tpu_custom_call" | custom-call | tf_op jit(solution)/shard_map/backward/pallas_call | solution.py:1603
  299.4 0.0 copy-start.1
  299.4 0.0 copy-start
  299.5 0.0 copy-start.3
  299.5 10.0 %widen.1 = f32[576,7000]{1,0:T(8,128)} custom-call(bf16[576,7168]{1,0:T(8,128)(2,1)} %get-tuple-element.48.a), custom_call_target="tpu_custom_call" | custom-call | bytes 24192000 | tf_op jit(solution)/shard_map/widen/pallas_call | solution.py:1649
  309.5 0.0 copy-start.5
  309.5 0.0 copy-start.7
  309.5 0.0 copy-start.6
  309.5 0.0 copy-start.8
  309.5 0.0 copy-done.1
  309.5 0.6 reshape.52
  310.1 0.0 copy-start.2
  310.1 0.3 dynamic_slice.3
  310.4 1.5 reshape.53
  311.8 0.0 copy-done
  311.8 0.1 slice.14
  311.9 1.3 reshape.56
  313.2 0.0 copy-done.3
  313.2 0.9 reshape.54
  314.1 1.2 slice.13
  315.4 2.0 copy.32
  317.4 0.0 copy-done.2
  317.4 0.7 copy.33
  318.1 0.0 copy-done.5
  318.1 0.6 copy.34
  318.7 0.0 copy-done.7
  318.7 0.6 copy.35
  319.3 0.0 copy-done.6
  319.3 0.6 copy.36
  319.9 0.0 copy-done.8
  319.9 0.6 copy.37
Async XLA Ops:
  1.9 58.8 %copy-start.4 = (f32[7000]{0:T(1024)S(1)}, f32[7000]{0:T(1024)}, u32[]{:S(2)}) copy-start(f32[7000]{0:T(1024)} %param.27) | copy-start | bytes 84004
  299.4 10.0 %copy-start.1 = (f32[224,800]{1,0:T(8,128)S(1)}, f32[224,800]{1,0:T(8,128)}, u32[]{:S(2)}) copy-start(f32[224,800]{1,0:T(8,128)} %get-tuple-element.49) | copy-start | bytes 2150404
  299.4 12.4 %copy-start = (f32[25,7168]{1,0:T(8,128)S(1)}, f32[25,7168]{1,0:T(8,128)}, u32[]{:S(2)}) copy-start(f32[25,7168]{1,0:T(8,128)} %get-tuple-element.54) | copy-start | bytes 2150404
  299.5 13.8 %copy-start.3 = (f32[56,800]{1,0:T(8,128)S(1)}, f32[56,800]{1,0:T(8,128)}, u32[]{:S(2)}) copy-start(f32[56,800]{1,0:T(8,128)} %get-tuple-element.50) | copy-start | bytes 537604
  309.5 8.7 %copy-start.5 = (f32[56,128]{1,0:T(8,128)S(1)}, f32[56,128]{1,0:T(8,128)}, u32[]{:S(2)}) copy-start(f32[56,128]{1,0:T(8,128)} %get-tuple-element.55) | copy-start | bytes 86020
  309.5 9.3 %copy-start.7 = (f32[4,800]{1,0:T(4,128)S(1)}, f32[4,800]{1,0:T(4,128)}, u32[]{:S(2)}) copy-start(f32[4,800]{1,0:T(4,128)} %get-tuple-element.78) | copy-start | bytes 38404
  309.5 9.9 %copy-start.6 = (f32[4,800]{1,0:T(4,128)S(1)}, f32[4,800]{1,0:T(4,128)}, u32[]{:S(2)}) copy-start(f32[4,800]{1,0:T(4,128)} %get-tuple-element.79) | copy-start | bytes 38404
  309.5 10.5 %copy-start.8 = (f32[4,100]{1,0:T(4,128)S(1)}, f32[4,100]{1,0:T(4,128)}, u32[]{:S(2)}) copy-start(f32[4,100]{1,0:T(4,128)} %get-tuple-element.58) | copy-start | bytes 4804
  310.1 7.3 %copy-start.2 = (f32[100,800]{1,0:T(8,128)S(1)}, f32[100,800]{1,0:T(8,128)}, u32[]{:S(2)}) copy-start(f32[100,800]{1,0:T(8,128)} %get-tuple-element.74) | copy-start | bytes 960004
